TPU v7x, 128 devices: a whole 4x4x4 slice. The times are simulated.
128 devices in a mesh: dp: 32 (over y, z, core), tp: 4 (over x).
Axes of the slice: x: 4, y: 4, z: 4, core: 2. Of those that a mesh axis runs over, the one named last changes fastest.
Arguments:
- latent_cache: bfloat16 [256, 448, 576], P('dp'), may hold values from -5 to 5
- lengths: int32 [256], replicated, may hold values from 1 to 446, as said below
- slot_moves: int32 [2, 32, 2], replicated, may hold values from 0 to 7, as said below
- hidden_in: bfloat16 [2, 256, 7168], P(None, 'dp', 'tp'), may hold values from -7.2 to 7.2
- queries: bfloat16 [2, 256, 128, 576], P(None, 'dp', 'tp'), may hold values from -6 to 6
- latent_weight: bfloat16 [7168, 576], P('tp'), may hold values from -0.0625 to 0.0625
- value_up_projection: bfloat16 [128, 512, 128], P('tp'), may hold values from -0.25 to 0.25
- out_weight: bfloat16 [16384, 7168], P('dp', 'tp'), may hold values from -0.046875 to 0.046875
- post_gain: float32 [7168], P('tp'), may hold values from 0.1 to 1.9
- gate_projection_matrix: bfloat16 [7168, 18432], P('tp', 'dp'), may hold values from -0.0625 to 0.0625
- up_weight: bfloat16 [7168, 18432], P('tp', 'dp'), may hold values from -0.0625 to 0.0625
- down_weight: bfloat16 [18432, 7168], P('dp', 'tp'), may hold values from -0.046875 to 0.046875
Outputs:
- layer_out: bfloat16 [2, 256, 7168], P(None, 'dp', 'tp')
- final_cache: bfloat16 [256, 448, 576], P('dp')
- final_lengths: int32 [256], replicated
Inputs may be any that keep to these rules, and one draw needn't show every extreme that they name: `lengths`: the largest length is 446 in every draw. `slot_moves`: for each step and group the two local slots differ.
All inputs are finite; a program needn't handle non-finite values.
Results may differ from a plain program's by a relative error of at most 0.015.
Values may be sent and summed in bfloat16 or wider, within the bound.
A program may use at most 128 MiB of HBM per device.

v0:
```python
import jax
import jax.numpy as jnp
from jax import lax
from jax.sharding import PartitionSpec as P

D = 7168
KVR = 512
ROPE = 64
HD = 128
STEPS = 2


epsilon = 1e-06


def shifted(block, axis, distance):
    devices = range(lax.axis_size(axis))
    route = [((i - distance) % len(devices), i) for i in devices]
    return lax.ppermute(block, axis, route)


def source_slots(moves_step, groups, per_group):
    group_base = jnp.arange(groups, dtype=jnp.int32) * per_group
    right_slot = group_base + moves_step[:, 0]
    left_slot = group_base + moves_step[:, 1]
    source = jnp.arange(groups * per_group, dtype=jnp.int32)
    source = source.at[right_slot].set(jnp.roll(left_slot, -1))
    source = source.at[left_slot].set(jnp.roll(right_slot, 1))
    return source


def rotate_pairs(rotary, positions):
    half_width = rotary.shape[-1] // 2
    frequencies = 10000.0 ** (-2.0 * jnp.arange(half_width, dtype=jnp.float32) / rotary.shape[-1])
    angles = positions.astype(jnp.float32)[:, None] * frequencies[None, :]
    cosine = jnp.cos(angles)
    sine_part = jnp.sin(angles)
    front_half = rotary[:, :half_width]
    back_half = rotary[:, half_width:]
    return jnp.concatenate(
        [front_half * cosine - back_half * sine_part, back_half * cosine + front_half * sine_part],
        axis=1,
    )


def finish_key(latent, positions):
    content = latent[:, :KVR]
    content = content * lax.rsqrt(jnp.mean(content * content, axis=1, keepdims=True) + epsilon)
    return jnp.concatenate([content, rotate_pairs(latent[:, KVR:], positions)], axis=1).astype(
        jnp.bfloat16
    )


def activate(gate_sum, up_sum, squared_entry_sum):
    row_scale = lax.rsqrt(squared_entry_sum / D + epsilon)[:, None]
    return (jax.nn.silu(gate_sum * row_scale) * (up_sum * row_scale)).astype(jnp.bfloat16)


def on_device(
    latent_cache,
    lengths,
    slot_moves,
    hidden_in,
    queries,
    latent_weight,
    value_up_projection,
    out_weight,
    post_gain,
    gate_projection_matrix,
    up_weight,
    down_weight,
):
    per_group = latent_cache.shape[0]
    capacity = latent_cache.shape[1]
    groups = lax.axis_size("dp")
    group_position_index = lax.axis_index("dp")
    score_scale = (HD + ROPE) ** (-0.5)
    slot_ids = jnp.arange(per_group, dtype=jnp.int32)
    positions = jnp.arange(capacity, dtype=jnp.int32)
    results = []
    for step_index in range(STEPS):
        source = source_slots(slot_moves[step_index], groups, per_group)
        held_lengths = lengths[source]
        own_moves = lax.dynamic_index_in_dim(
            slot_moves[step_index], group_position_index, 0, keepdims=False
        )
        right_out = own_moves[0]
        left_out = own_moves[1]
        leaving_right = lax.dynamic_index_in_dim(latent_cache, right_out, 0, keepdims=False)
        leaving_left = lax.dynamic_index_in_dim(latent_cache, left_out, 0, keepdims=False)
        from_left = shifted(leaving_right, "dp", 1)
        from_right = shifted(leaving_left, "dp", -1)
        latent_cache = lax.dynamic_update_index_in_dim(latent_cache, from_left, left_out, 0)
        latent_cache = lax.dynamic_update_index_in_dim(latent_cache, from_right, right_out, 0)
        own_lengths = lax.dynamic_slice_in_dim(
            held_lengths, group_position_index * per_group, per_group
        )
        tokens = hidden_in[step_index]
        tokens_wide = tokens.astype(jnp.float32)
        partial_latent = jnp.dot(tokens, latent_weight, preferred_element_type=jnp.float32)
        latent_sum, squared_entry_sum = lax.psum(
            (partial_latent, jnp.sum(tokens_wide * tokens_wide, axis=1)), "tp"
        )
        latent = latent_sum * lax.rsqrt(squared_entry_sum / D + epsilon)[:, None]
        fresh_key = finish_key(latent, own_lengths)
        latent_cache = latent_cache.at[slot_ids, own_lengths].set(fresh_key)
        lengths = held_lengths + 1
        visible = positions[None, :] < (own_lengths + 1)[:, None]
        scores = (
            jnp.einsum(
                "rhl,rtl->rht",
                queries[step_index],
                latent_cache,
                preferred_element_type=jnp.float32,
            )
            * score_scale
        )
        scores = jnp.where(visible[:, None, :], scores, -1e30)
        peak_score = jnp.max(scores, axis=2, keepdims=True)
        powers = jnp.exp(scores - peak_score)
        weights = (powers / jnp.sum(powers, axis=2, keepdims=True)).astype(jnp.bfloat16)
        per_head_latent_vector = jnp.einsum(
            "rht,rtk->rhk", weights, latent_cache[:, :, :KVR], preferred_element_type=jnp.float32
        ).astype(jnp.bfloat16)
        head_output_rows = jnp.einsum(
            "gfe,feu->gfu",
            per_head_latent_vector,
            value_up_projection,
            preferred_element_type=jnp.float32,
        ).astype(jnp.bfloat16)
        head_output_rows = head_output_rows.reshape(per_group, -1)
        all_heads = lax.all_gather(head_output_rows, "tp", axis=1, tiled=True)
        head_block = lax.all_to_all(all_heads, "dp", split_axis=1, concat_axis=0, tiled=True)
        attention = lax.psum_scatter(
            jnp.dot(head_block, out_weight, preferred_element_type=jnp.float32),
            "dp",
            scatter_dimension=0,
            tiled=True,
        )
        mixed_rows = (tokens_wide + attention).astype(jnp.bfloat16)
        mixed_all = lax.all_gather(mixed_rows, "dp", axis=0, tiled=True)
        mixed_wide = mixed_all.astype(jnp.float32)
        scaled = (mixed_wide * post_gain).astype(jnp.bfloat16)
        gate_part = jnp.dot(scaled, gate_projection_matrix, preferred_element_type=jnp.float32)
        up_part = jnp.dot(scaled, up_weight, preferred_element_type=jnp.float32)
        square_part = jnp.sum(mixed_wide * mixed_wide, axis=1)
        gate_sum, up_sum, norm_sum = lax.psum((gate_part, up_part, square_part), "tp")
        activation = activate(gate_sum, up_sum, norm_sum)
        down_sum = lax.psum_scatter(
            jnp.dot(activation, down_weight, preferred_element_type=jnp.float32).astype(
                jnp.bfloat16
            ),
            "dp",
            scatter_dimension=0,
            tiled=True,
        ).astype(jnp.float32)
        results.append((mixed_rows.astype(jnp.float32) + down_sum).astype(jnp.bfloat16))
    return (jnp.stack(results), latent_cache, lengths)


def solution(mesh):
    return jax.shard_map(
        on_device,
        mesh=mesh,
        in_specs=(
            P("dp", None, None),
            P(),
            P(),
            P(None, "dp", "tp"),
            P(None, "dp", "tp", None),
            P("tp", None),
            P("tp", None, None),
            P("dp", "tp"),
            P("tp"),
            P("tp", "dp"),
            P("tp", "dp"),
            P("dp", "tp"),
        ),
        out_specs=(P(None, "dp", "tp"), P("dp", None, None), P()),
        check_vma=False,
    )
```

profile of v0, /device:TPU:1, one launch (start us, length us, event | category | flops | bytes accessed | tf_op | source)
XLA Modules:
  0.0 545.8 jit_solution(1939577747678407836)
XLA Ops:
  7.2 5.0 copy.36
  35.7 14.0 %all-reduce.1 = (f32[8,576]{1,0:T(8,128)S(1)}, f32[8]{0:T(128)S(1)}, f32[8,576]{1,0:T(8,128)S(1)}, f32[8]{0:T(128)S(1)}) all-reduce(f32[8,576]{1,0:T(8,128)S(1)} %fusion.50, f32[8]{0:T(128)S(1)} %get-tuple-element.4, f32[8,576]{1,0:T(8,128)S(1)} %fusion.48, f32[8]{0:T(128)S(1)} %get-tuple-element.3), channel_id=1, replica_groups=mesh['dp'=32,'tp'=4] {'tp'}, use_global_device_ids=true, to_apply=%region_2.3 | all-reduce | flops 9232 | bytes 73856 | tf_op jit(solution)/shard_map/psum | solution.py:101
  60.3 3.8 fusion.15
  64.3 3.5 fusion.4
  70.8 10.1 %all_gather.12 = bf16[8,16384]{1,0:T(8,128)(2,1)} all-gather(bf16[8,4096]{1,0:T(8,128)(2,1)S(1)} %fusion.19), channel_id=1, replica_groups=mesh['dp'=32,'tp'=4] {'tp'}, dimensions={1}, use_global_device_ids=true | all-gather | bytes 327680 | tf_op jit(solution)/shard_map/all_gather | solution.py:132
  81.0 14.3 %all-to-all-start = ((bf16[8,32,512]{2,0,1:T(8,128)(2,1)}), bf16[8,32,512]{2,0,1:T(8,128)(2,1)S(1)}, u32[]{:S(2)}, u32[]{:S(2)}) async-start(bf16[8,32,512]{2,0,1:T(8,128)(2,1)} %bitcast.18), calls=%async_computation | async-start | bytes 524288 | tf_op jit(solution)/shard_map/all_to_all | solution.py:133
  98.9 5.6 %all-to-all-done = bf16[8,32,512]{2,0,1:T(8,128)(2,1)S(1)} async-done(((bf16[8,32,512]{2,0,1:T(8,128)(2,1)}), bf16[8,32,512]{2,0,1:T(8,128)(2,1)S(1)}, u32[]{:S(2)}, u32[]{:S(2)}) %all-to-all-start) | async-done | bytes 262176 | tf_op jit(solution)/shard_map/all_to_all | solution.py:133
  104.4 3.4 fusion.38
  110.1 3.1 collective-permute-start.3
  113.4 5.8 %collective-permute-done.3 = bf16[448,576]{1,0:T(8,128)(2,1)S(1)} collective-permute-done((bf16[448,576]{1,0:T(8,128)(2,1)S(1)}, bf16[448,576]{1,0:T(8,128)(2,1)S(1)}, u32[]{:S(2)}, u32[]{:S(2)}) %collective-permute-start.3) | collective-permute-done | bytes 516128 | tf_op jit(solution)/shard_map/ppermute | solution.py:19
  122.3 3.8 fusion.13
  129.3 3.1 fusion.18
  132.4 9.4 %all_gather.14 = bf16[8,16384]{1,0:T(8,128)(2,1)S(1)} all-gather(bf16[8,4096]{1,0:T(8,128)(2,1)S(1)} %fusion.18), channel_id=1, replica_groups=mesh['dp'=32,'tp'=4] {'tp'}, dimensions={1}, use_global_device_ids=true | all-gather | bytes 327680 | tf_op jit(solution)/shard_map/all_gather | solution.py:132
  141.7 17.7 %all_to_all.38 = bf16[8,32,512]{2,0,1:T(8,128)(2,1)S(1)} all-to-all(bf16[8,32,512]{2,0,1:T(8,128)(2,1)S(1)} %bitcast.128), channel_id=1, replica_groups=mesh['dp'=32,'tp'=4] {'dp'}, dimensions={1} | all-to-all | bytes 524288 | tf_op jit(solution)/shard_map/all_to_all | solution.py:133
  161.4 20.6 %reduce-scatter.5.cloned.1.call-done = f32[8,1792]{1,0:T(8,128)} async-done(((f32[256,1792]{1,0:T(8,128)}), f32[8,1792]{1,0:T(8,128)}) %reduce-scatter.5.cloned.1.call-update) | async-done | bytes 57360 | tf_op jit(solution)/shard_map/reduce_scatter | solution.py:134
  181.9 81.4 %reduce-scatter.9.cloned.1.call-done = f32[8,1792]{1,0:T(8,128)} async-done(((f32[256,1792]{1,0:T(8,128)}), f32[8,1792]{1,0:T(8,128)}) %reduce-scatter.9.cloned.1.call-update) | async-done | bytes 57360 | tf_op jit(solution)/shard_map/reduce_scatter | solution.py:134
  264.3 26.3 %all_gather.13 = bf16[256,1792]{1,0:T(8,128)(2,1)S(1)} all-gather(bf16[8,1792]{1,0:T(8,128)(2,1)S(1)} %get-tuple-element.19), channel_id=1, replica_groups=mesh['dp'=32,'tp'=4] {'dp'}, dimensions={0}, use_global_device_ids=true | all-gather | bytes 946176 | tf_op jit(solution)/shard_map/all_gather | solution.py:141
  290.6 3.3 fusion.24
  295.5 22.7 %all_gather.15 = bf16[256,1792]{1,0:T(8,128)(2,1)S(1)} all-gather(bf16[8,1792]{1,0:T(8,128)(2,1)S(1)} %get-tuple-element.20), channel_id=1, replica_groups=mesh['dp'=32,'tp'=4] {'dp'}, dimensions={0}, use_global_device_ids=true | all-gather | bytes 946176 | tf_op jit(solution)/shard_map/all_gather | solution.py:141
  323.1 8.4 %all-reduce = (f32[256]{0:T(256)S(1)}, f32[256]{0:T(256)S(1)}) all-reduce(f32[256]{0:T(256)S(1)} %fusion.9, f32[256]{0:T(256)S(1)} %fusion.7), channel_id=1, replica_groups=mesh['dp'=32,'tp'=4] {'tp'}, use_global_device_ids=true, to_apply=%region_27.28 | all-reduce | flops 512 | bytes 4096 | tf_op jit(solution)/shard_map/psum | solution.py:147
  331.5 52.1 %all-reduce.5.cloned.1.call-done = (f32[256,576]{0,1:T(8,128)}, f32[256,576]{0,1:T(8,128)}, f32[256,576]{0,1:T(8,128)}, f32[256,576]{0,1:T(8,128)}) async-done(((f32[256,576]{0,1:T(8,128)}, f32[256,576]{0,1:T(8,128)}, f32[256,576]{0,1:T(8,128)}, f32[256,576]{0,1:T(8,128)}), (f32[256,576]{0,1:T(8,128)}, f32[256,576]{0,1:T(8,128)}, f32[256,576]{0,1:T(8,128)}, ...) | async-done | bytes 2359312 | tf_op jit(solution)/shard_map/psum | solution.py:147
  383.6 3.2 convolution_convert_fusion.1
  390.4 69.7 %reduce-scatter.7.cloned.1.call-done = bf16[8,1792]{1,0:T(8,128)(2,1)} async-done(((bf16[256,1792]{1,0:T(8,128)(2,1)}), bf16[8,1792]{1,0:T(8,128)(2,1)}) %reduce-scatter.7.cloned.1.call-update) | async-done | bytes 28688 | tf_op jit(solution)/shard_map/reduce_scatter | solution.py:149
  460.9 77.0 %reduce-scatter.11.cloned.1.call-done = bf16[8,1792]{1,0:T(8,128)(2,1)} async-done(((bf16[256,1792]{1,0:T(8,128)(2,1)}), bf16[8,1792]{1,0:T(8,128)(2,1)}) %reduce-scatter.11.cloned.1.call-update) | async-done | bytes 28688 | tf_op jit(solution)/shard_map/reduce_scatter | solution.py:149
  (115 shorter events, 56.9 us)
Async XLA Ops:
  7.2 376.4 %copy-start = (bf16[576,1792]{1,0:T(8,128)(2,1)S(1)}, bf16[576,1792]{1,0:T(8,128)(2,1)}, u32[]{:S(2)}) copy-start(bf16[576,1792]{1,0:T(8,128)(2,1)} %param.23) | copy-start | bytes 6193156
  7.2 5.0 copy-start.7
  12.2 9.9 %copy-start.6 = (bf16[2,8,1792]{2,1,0:T(8,128)(2,1)S(1)}, bf16[2,8,1792]{2,1,0:T(8,128)(2,1)}, u32[]{:S(2)}) copy-start(bf16[2,8,1792]{2,1,0:T(8,128)(2,1)} %param.15) | copy-start | bytes 172036
  19.0 37.2 %collective-permute-start.1 = (bf16[448,576]{1,0:T(8,128)(2,1)}, bf16[448,576]{1,0:T(8,128)(2,1)}, u32[]{:S(2)}, u32[]{:S(2)}) collective-permute-start(bf16[448,576]{1,0:T(8,128)(2,1)} %get-tuple-element.17), channel_id=1, source_target_pairs={{4,0},{8,4},{12,8},{16,12},{20,16},{24,20},{28,24},{32,28},{36,32}... | collective-permute-start | bytes 1548296 | tf_op jit(solution)/shard_map/ppermute | solution.py:19
  20.4 33.8 %collective-permute-start = (bf16[448,576]{1,0:T(8,128)(2,1)}, bf16[448,576]{1,0:T(8,128)(2,1)}, u32[]{:S(2)}, u32[]{:S(2)}) collective-permute-start(bf16[448,576]{1,0:T(8,128)(2,1)} %get-tuple-element.18), channel_id=1, source_target_pairs={{124,0},{0,4},{4,8},{8,12},{12,16},{16,20},{20,24},{24,28},{28,32}... | collective-permute-start | bytes 1548296 | tf_op jit(solution)/shard_map/ppermute | solution.py:19
  22.0 2.5 copy-start.2
  27.9 3.7 copy-start.1
  33.5 26.8 %copy-start.5 = (bf16[2,8,32,576]{3,2,1,0:T(8,128)(2,1)S(1)}, bf16[2,8,32,576]{3,2,1,0:T(8,128)(2,1)}, u32[]{:S(2)}) copy-start(bf16[2,8,32,576]{3,2,1,0:T(8,128)(2,1)} %param.16) | copy-start | bytes 1769476
  81.0 23.5 %all-to-all-start = ((bf16[8,32,512]{2,0,1:T(8,128)(2,1)}), bf16[8,32,512]{2,0,1:T(8,128)(2,1)S(1)}, u32[]{:S(2)}, u32[]{:S(2)}) async-start(bf16[8,32,512]{2,0,1:T(8,128)(2,1)} %bitcast.18), calls=%async_computation | async-start | bytes 524288 | tf_op jit(solution)/shard_map/all_to_all | solution.py:133
  95.2 86.7 %reduce-scatter.5.cloned.1.call-start = ((), (), s32[]{:S(2)}) async-start(), calls=%async_computation.6 | async-start | bytes 1892352 | tf_op jit(solution)/shard_map/reduce_scatter | solution.py:134
  97.2 10.7 %collective-permute-start.2 = (bf16[448,576]{1,0:T(8,128)(2,1)}, bf16[448,576]{1,0:T(8,128)(2,1)}, u32[]{:S(2)}, u32[]{:S(2)}) collective-permute-start(bf16[448,576]{1,0:T(8,128)(2,1)} %dynamic-slice_bitcast_fusion.1), channel_id=1, source_target_pairs={{124,0},{0,4},{4,8},{8,12},{12,16},{16,20},{20,24},{24,28},{28,32}... | collective-permute-start | bytes 1548296 | tf_op jit(solution)/shard_map/ppermute | solution.py:19
  107.9 155.5 %reduce-scatter.9.cloned.1.call-start = ((), (), s32[]{:S(2)}) async-start(), calls=%async_computation.8 | async-start | bytes 1892352 | tf_op jit(solution)/shard_map/reduce_scatter | solution.py:134
  110.1 9.1 %collective-permute-start.3 = (bf16[448,576]{1,0:T(8,128)(2,1)S(1)}, bf16[448,576]{1,0:T(8,128)(2,1)S(1)}, u32[]{:S(2)}, u32[]{:S(2)}) collective-permute-start(bf16[448,576]{1,0:T(8,128)(2,1)S(1)} %get-tuple-element.15), channel_id=1, source_target_pairs={{4,0},{8,4},{12,8},{16,12},{20,16},{24,20},{28,24},{32,28},{36,32}... | collective-permute-start | bytes 1548296 | tf_op jit(solution)/shard_map/ppermute | solution.py:19
  129.2 30.2 %copy-start.3 = (bf16[512,1792]{1,0:T(8,128)(2,1)S(1)}, bf16[512,1792]{1,0:T(8,128)(2,1)}, u32[]{:S(2)}) copy-start(bf16[512,1792]{1,0:T(8,128)(2,1)} %param.19) | copy-start | bytes 5505028
  161.3 129.3 %copy-start.11 = (f32[1792]{0:T(1024)S(1)}, f32[1792]{0:T(1024)}, u32[]{:S(2)}) copy-start(f32[1792]{0:T(1024)} %param.20) | copy-start | bytes 21508
  161.3 222.2 %all-reduce.5.cloned.1.call-start = ((), (), s32[]{:S(2)}) async-start(), calls=%async_computation.10 | async-start | bytes 4718592 | tf_op jit(solution)/shard_map/psum | solution.py:147
  290.6 3.3 copy-start.9
  293.9 24.3 %copy-start.8 = (bf16[1792,576]{0,1:T(8,128)(2,1)S(1)}, bf16[1792,576]{0,1:T(8,128)(2,1)}, u32[]{:S(2)}) copy-start(bf16[1792,576]{0,1:T(8,128)(2,1)} %param.22) | copy-start | bytes 6193156
  318.2 1.6 copy-start.4
  321.3 138.8 %reduce-scatter.7.cloned.1.call-start = ((), (), s32[]{:S(2)}) async-start(), calls=%async_computation.7 | async-start | bytes 946176 | tf_op jit(solution)/shard_map/reduce_scatter | solution.py:149
  383.6 3.3 copy-start.10
  386.8 151.1 %reduce-scatter.11.cloned.1.call-start = ((), (), s32[]{:S(2)}) async-start(), calls=%async_computation.9 | async-start | bytes 946176 | tf_op jit(solution)/shard_map/reduce_scatter | solution.py:149
Sparse Core Ops, SparseCore 0:
  108.0 73.9 reduce-scatter.4
  185.5 77.8 reduce-scatter.8
  321.5 62.0 all-reduce.4
  387.0 73.1 reduce-scatter.6
  463.6 74.2 reduce-scatter.10
where the time goes:
time: 548 us; the launch traced here: 546 us
  waiting for transfers between devices  312 us (57%)
  blocking collectives  109 us (20%)
  matrix products  42.6 us (8%)
  local copies, waits for them, and re-layouts  29.7 us (5%)
  starting transfers between devices  22.2 us (4%)
  between operations  21.6 us (4%)
  other arithmetic  8.83 us (2%)
    reduce_scatter x2, waiting for transfers between devices, on_device(): lax.psum_scatter(jnp.dot(activation, down_weight, preferred_element_type=...  147 us
    reduce_scatter x2, waiting for transfers between devices, on_device(): lax.psum_scatter(jnp.dot(head_block, out_weight, preferred_element_type=j...  102 us
    psum x1, waiting for transfers between devices, on_device(): lax.psum((gate_part, up_part, square_part), 'tp')  52.1 us
    all_gather x2, blocking collectives, on_device(): mixed_all = lax.all_gather(mixed_rows, 'dp', axis=0, tiled=True)  49.1 us
    all_gather x2, blocking collectives, on_device(): all_heads = lax.all_gather(head_output_rows, 'tp', axis=1, tiled=True)  19.5 us
    all_to_all x1, blocking collectives, on_device(): lax.all_to_all(all_heads, 'dp', split_axis=1, concat_axis=0, tiled=True)  17.7 us
    all_to_all x1, starting transfers between devices, on_device(): lax.all_to_all(all_heads, 'dp', split_axis=1, concat_axis=0, tiled=True)  14.3 us
    psum x1, blocking collectives, on_device(): lax.psum((partial_latent, jnp.sum(tokens_wide * tokens_wide, axis=1)), 'tp')  14 us
  transfers between devices with their start and end apart: 10, of which 7 were waited for; matrix products, arithmetic and copies ran while one was open for 8% of the time, Pallas kernels for 0%

commit v1 on v0

--- a/solution.py
+++ b/solution.py
@@ -1,6 +1,10 @@
+import functools
+
 import jax
 import jax.numpy as jnp
 from jax import lax
+from jax.experimental import pallas as pl
+from jax.experimental.pallas import tpu as pltpu
 from jax.sharding import PartitionSpec as P
 
 D = 7168
@@ -8,6 +12,14 @@
 ROPE = 64
 HD = 128
 STEPS = 2
+ROWS_DEV = 8
+N = 4
+OWN = STEPS * ROWS_DEV
+HALF = N * N * OWN
+WIDTH = D // N
+FF_DEV = 576
+CHUNK = 2 * HALF // N
+MESH = pl.DeviceIdType.MESH
 
 
 epsilon = 1e-06
@@ -51,9 +63,349 @@
     )
 
 
-def activate(gate_sum, up_sum, squared_entry_sum):
-    row_scale = lax.rsqrt(squared_entry_sum / D + epsilon)[:, None]
-    return (jax.nn.silu(gate_sum * row_scale) * (up_sum * row_scale)).astype(jnp.bfloat16)
+class Place:
+    def __init__(self):
+        dp = lax.axis_index("dp")
+        self.x = lax.axis_index("tp")
+        self.y = dp // (2 * N)
+        self.z = (dp // 2) % N
+        self.c = dp % 2
+        self.first = self.c * self.y + (1 - self.c) * self.z
+        self.second = self.c * self.z + (1 - self.c) * self.y
+
+    def group(self, y, z, c):
+        return y * (2 * N) + z * 2 + c
+
+    def on_first(self, k):
+        y = self.c * k + (1 - self.c) * self.y
+        z = self.c * self.z + (1 - self.c) * k
+        return {"dp": self.group(y, z, self.c), "tp": self.x}
+
+    def on_second(self, k):
+        y = self.c * self.y + (1 - self.c) * k
+        z = self.c * k + (1 - self.c) * self.z
+        return {"dp": self.group(y, z, self.c), "tp": self.x}
+
+    def on_core(self):
+        return {"dp": self.group(self.y, self.z, 1 - self.c), "tp": self.x}
+
+    def on_x(self, k):
+        return {"dp": self.group(self.y, self.z, self.c), "tp": k}
+
+
+def send(src, dst, send_sem, recv_sem, device):
+    copy = pltpu.make_async_remote_copy(
+        src_ref=src,
+        dst_ref=dst,
+        send_sem=send_sem,
+        recv_sem=recv_sem,
+        device_id=device,
+        device_id_type=MESH,
+    )
+    copy.start()
+    return copy
+
+
+def reduce_over_groups(here, to_peer, own, sums, parts, peer_rows, rows1, rows2, sems):
+    core_sem, sem1, sem2 = sems
+    core = pltpu.make_async_remote_copy(
+        src_ref=to_peer,
+        dst_ref=peer_rows,
+        send_sem=core_sem.at[0],
+        recv_sem=core_sem.at[1],
+        device_id=here.on_core(),
+        device_id_type=MESH,
+    )
+    core.wait()
+    copies = []
+    for o in (2, 1, 3):
+        k = lax.rem(here.first + o, N)
+        rows = pl.ds(pl.multiple_of(k * N * OWN, N * OWN), N * OWN)
+        sums[k] = (
+            own[rows, :].astype(jnp.float32) + peer_rows[rows, :].astype(jnp.float32)
+        ).astype(jnp.bfloat16)
+        copies.append(
+            send(sums.at[k], rows1.at[o - 1], sem1.at[0, o - 1], sem1.at[1, o - 1], here.on_first(k))
+        )
+    for copy in copies:
+        copy.wait()
+    rows = pl.ds(pl.multiple_of(here.first * N * OWN, N * OWN), N * OWN)
+    total = own[rows, :].astype(jnp.float32) + peer_rows[rows, :].astype(jnp.float32)
+    for o in range(N - 1):
+        total = total + rows1[o].astype(jnp.float32)
+    parts[...] = total.astype(jnp.bfloat16).reshape(parts.shape)
+    copies = []
+    for o in (2, 1, 3):
+        k = lax.rem(here.second + o, N)
+        copies.append(
+            send(parts.at[k], rows2.at[o - 1], sem2.at[0, o - 1], sem2.at[1, o - 1], here.on_second(k))
+        )
+    for copy in copies:
+        copy.wait()
+    total = parts[here.second].astype(jnp.float32)
+    for o in range(N - 1):
+        total = total + rows2[o].astype(jnp.float32)
+    return total
+
+
+def multiply(lhs, weight, out, first_row, rows):
+    tile = 256
+
+    @pl.loop(0, WIDTH // tile)
+    def _(i):
+        columns = pl.ds(pl.multiple_of(i * tile, tile), tile)
+        out[:, columns] = jnp.dot(
+            lhs[pl.ds(first_row, rows), :], weight[:, columns], preferred_element_type=jnp.float32
+        ).astype(jnp.bfloat16)
+
+
+def back_kernel(
+    heads, tokens, gain, wo_hbm, wg_hbm, wu_hbm, wd_hbm,
+    out,
+    wo, wg, wu, wd, head_rows, head_block,
+    to_peer, own, peer_a, peer_d, sums, parts, rows1_a, rows1_d, rows2_a, rows2_d,
+    norms, norm_rows, mixed_all, gate_part, up_part, gate_rows, up_rows, activation,
+    weight_sem, head_send, head_recv, core_a, sem1_a, sem2_a, core_d, sem1_d, sem2_d,
+    norm_sem, gather2, gather1, gather_core, gate_sem, up_sem, act_sem,
+):
+    here = Place()
+    loads = []
+    for i, (src, dst) in enumerate(((wo_hbm, wo), (wg_hbm, wg), (wu_hbm, wu), (wd_hbm, wd))):
+        load = pltpu.make_async_copy(src, dst, weight_sem.at[i])
+        load.start()
+        loads.append(load)
+
+    barrier = pltpu.get_barrier_semaphore()
+    pl.semaphore_signal(barrier, inc=1, device_id=here.on_core(), device_id_type=MESH)
+    for o in range(1, N):
+        for device in (
+            here.on_first(lax.rem(here.first + o, N)),
+            here.on_second(lax.rem(here.second + o, N)),
+            here.on_x(lax.rem(here.x + o, N)),
+        ):
+            pl.semaphore_signal(barrier, inc=1, device_id=device, device_id_type=MESH)
+
+    me = here.group(here.y, here.z, here.c)
+
+    @pl.loop(0, 2 * N * N)
+    def _(i):
+        d = lax.rem(me + i, 2 * N * N)
+
+        @pl.when((d != me) | (here.x != here.y))
+        def _():
+            pl.semaphore_signal(barrier, inc=1, device_id={"dp": d, "tp": here.y}, device_id_type=MESH)
+
+    away = jnp.where(here.x == here.y, 0, 1)
+    pl.semaphore_wait(barrier, 1 + 3 * (N - 1) + 2 * N * N - 1 + away)
+
+    place = here.c * (N * N) + here.first * N + here.second
+    k_me = here.z * 2 + here.c
+
+    def head_copy(i):
+        k = lax.rem(k_me + i // N, 2 * N)
+        x = lax.rem(here.x + i, N)
+        return k, x, pltpu.make_async_remote_copy(
+            src_ref=heads.at[k],
+            dst_ref=head_rows.at[place],
+            send_sem=head_send.at[i],
+            recv_sem=head_recv.at[place],
+            device_id={"dp": here.x * (2 * N) + k, "tp": x},
+            device_id_type=MESH,
+        )
+
+    kept = pltpu.make_async_copy(heads.at[k_me], head_rows.at[place], head_recv.at[place])
+
+    @pl.loop(0, 2 * N * N)
+    def _(i):
+        k, x, copy = head_copy(i)
+
+        @pl.when((x == here.x) & (k == k_me) & (here.x == here.y))
+        def _():
+            kept.start()
+
+        @pl.when((x != here.x) | (k != k_me) | (here.x != here.y))
+        def _():
+            copy.start()
+
+    @pl.loop(0, 2 * N * N)
+    def _(i):
+        pltpu.make_async_copy(heads.at[0], head_rows.at[i], head_recv.at[i]).wait()
+
+    @pl.loop(0, 2 * N * N)
+    def _(i):
+        k, x, copy = head_copy(i)
+
+        @pl.when((x != here.x) | (k != k_me) | (here.x != here.y))
+        def _():
+            copy.wait_send()
+
+    for h in range(N):
+        head_block[:, h * HD : (h + 1) * HD] = head_rows[:, h].reshape(2 * HALF, HD)
+
+    other_row = pl.multiple_of((1 - here.c) * HALF, HALF)
+    own_row = pl.multiple_of(here.c * HALF, HALF)
+    loads[0].wait()
+    multiply(head_block, wo, to_peer, other_row, HALF)
+    send(to_peer, peer_a, core_a.at[0], core_a.at[1], here.on_core())
+    multiply(head_block, wo, own, own_row, HALF)
+    attention = reduce_over_groups(
+        here, to_peer, own, sums, parts, peer_a, rows1_a, rows2_a, (core_a, sem1_a, sem2_a)
+    )
+    mixed = (tokens[...].astype(jnp.float32) + attention).astype(jnp.bfloat16).astype(jnp.float32)
+
+    norms[...] = jnp.broadcast_to(jnp.sum(mixed * mixed, axis=1, keepdims=True), norms.shape)
+    copies = []
+    for o in (2, 1, 3):
+        x = lax.rem(here.x + o, N)
+        copies.append(
+            send(norms, norm_rows.at[o - 1], norm_sem.at[0, o - 1], norm_sem.at[1, o - 1], here.on_x(x))
+        )
+    for copy in copies:
+        copy.wait()
+    squares = norms[...]
+    for o in range(N - 1):
+        squares = squares + norm_rows[o]
+    scale = lax.rsqrt(squares / D + epsilon)[:, :1]
+    mixed_all[here.c, here.first, here.second] = (mixed * gain[...] * scale).astype(jnp.bfloat16)
+
+    mine = mixed_all.at[here.c, here.first, here.second]
+    copies = []
+    for o in (2, 1, 3):
+        k = lax.rem(here.second + o, N)
+        copies.append(send(mine, mine, gather2.at[0, o - 1], gather2.at[1, o - 1], here.on_second(k)))
+    for copy in copies:
+        copy.wait()
+    mine = mixed_all.at[here.c, here.first]
+    copies = []
+    for o in (2, 1, 3):
+        k = lax.rem(here.first + o, N)
+        copies.append(send(mine, mine, gather1.at[0, o - 1], gather1.at[1, o - 1], here.on_first(k)))
+    handed = [send(mine, mine, gather_core.at[0, 0], gather_core.at[1, 0], here.on_core())]
+    for o, copy in zip((2, 1, 3), copies):
+        copy.wait()
+        block = mixed_all.at[here.c, lax.rem(here.first + N - o, N)]
+        handed.append(send(block, block, gather_core.at[0, o], gather_core.at[1, o], here.on_core()))
+
+    loads[1].wait()
+    loads[2].wait()
+
+    def chunk_of(i):
+        return 2 * lax.rem(here.c + i // 2, 2) + lax.rem(here.x + i, 2)
+
+    def chunk_copies(k):
+        o = lax.rem(k - here.x + N, N)
+        slot = o - 1
+        return [
+            pltpu.make_async_remote_copy(
+                src_ref=part.at[k],
+                dst_ref=rows.at[slot],
+                send_sem=sem.at[0, slot],
+                recv_sem=sem.at[1, slot],
+                device_id=here.on_x(k),
+                device_id_type=MESH,
+            )
+            for part, rows, sem in ((gate_part, gate_rows, gate_sem), (up_part, up_rows, up_sem))
+        ]
+
+    for i in range(N):
+        if i == 2:
+            for copy in handed:
+                copy.wait()
+        k = chunk_of(i)
+        lhs = mixed_all[k // 2, pl.ds(2 * lax.rem(k, 2), 2)].reshape(CHUNK, WIDTH)
+        gate_part[k] = jnp.dot(lhs, wg[...], preferred_element_type=jnp.float32).astype(jnp.bfloat16)
+        up_part[k] = jnp.dot(lhs, wu[...], preferred_element_type=jnp.float32).astype(jnp.bfloat16)
+
+        @pl.when(k != here.x)
+        def _():
+            for copy in chunk_copies(k):
+                copy.start()
+
+    for o in range(1, N):
+        for copy in chunk_copies(lax.rem(here.x + o, N)):
+            copy.wait()
+    gate = gate_part[here.x].astype(jnp.float32)
+    up = up_part[here.x].astype(jnp.float32)
+    for o in range(N - 1):
+        gate = gate + gate_rows[o].astype(jnp.float32)
+        up = up + up_rows[o].astype(jnp.float32)
+    activation[here.x] = (gate / (1.0 + jnp.exp(-gate)) * up).astype(jnp.bfloat16)
+    mine = activation.at[here.x]
+    copies = []
+    for o in (2, 1, 3):
+        x = lax.rem(here.x + o, N)
+        copies.append(send(mine, mine, act_sem.at[0, o - 1], act_sem.at[1, o - 1], here.on_x(x)))
+    for copy in copies:
+        copy.wait()
+
+    loads[3].wait()
+    act_rows = activation.reshape(2 * HALF, FF_DEV)
+    multiply(act_rows, wd, to_peer, other_row, HALF)
+    send(to_peer, peer_d, core_d.at[0], core_d.at[1], here.on_core())
+    multiply(act_rows, wd, own, own_row, HALF)
+    down = reduce_over_groups(
+        here, to_peer, own, sums, parts, peer_d, rows1_d, rows2_d, (core_d, sem1_d, sem2_d)
+    )
+    out[...] = (mixed + down).astype(jnp.bfloat16)
+
+
+def back(heads, tokens, gain, wo, wg, wu, wd):
+    bf16, f32 = jnp.bfloat16, jnp.float32
+    vmem = pl.BlockSpec(memory_space=pltpu.VMEM)
+    hbm = pl.BlockSpec(memory_space=pl.ANY)
+    dma = pltpu.SemaphoreType.DMA
+    return pl.pallas_call(
+        back_kernel,
+        out_shape=jax.ShapeDtypeStruct((OWN, WIDTH), bf16),
+        in_specs=[vmem, vmem, vmem, hbm, hbm, hbm, hbm],
+        out_specs=vmem,
+        scratch_shapes=[
+            pltpu.VMEM(wo.shape, bf16),
+            pltpu.VMEM(wg.shape, bf16),
+            pltpu.VMEM(wu.shape, bf16),
+            pltpu.VMEM(wd.shape, bf16),
+            pltpu.VMEM((2 * N * N, N, OWN, HD), bf16),
+            pltpu.VMEM((2 * HALF, N * HD), bf16),
+            pltpu.VMEM((HALF, WIDTH), bf16),
+            pltpu.VMEM((HALF, WIDTH), bf16),
+            pltpu.VMEM((HALF, WIDTH), bf16),
+            pltpu.VMEM((HALF, WIDTH), bf16),
+            pltpu.VMEM((N, N * OWN, WIDTH), bf16),
+            pltpu.VMEM((N, OWN, WIDTH), bf16),
+            pltpu.VMEM((N - 1, N * OWN, WIDTH), bf16),
+            pltpu.VMEM((N - 1, N * OWN, WIDTH), bf16),
+            pltpu.VMEM((N - 1, OWN, WIDTH), bf16),
+            pltpu.VMEM((N - 1, OWN, WIDTH), bf16),
+            pltpu.VMEM((OWN, 128), f32),
+            pltpu.VMEM((N - 1, OWN, 128), f32),
+            pltpu.VMEM((2, N, N, OWN, WIDTH), bf16),
+            pltpu.VMEM((N, CHUNK, FF_DEV), bf16),
+            pltpu.VMEM((N, CHUNK, FF_DEV), bf16),
+            pltpu.VMEM((N - 1, CHUNK, FF_DEV), bf16),
+            pltpu.VMEM((N - 1, CHUNK, FF_DEV), bf16),
+            pltpu.VMEM((N, CHUNK, FF_DEV), bf16),
+            dma((4,)),
+            dma((2 * N * N,)),
+            dma((2 * N * N,)),
+            dma((2,)),
+            dma((2, N - 1)),
+            dma((2, N - 1)),
+            dma((2,)),
+            dma((2, N - 1)),
+            dma((2, N - 1)),
+            dma((2, N - 1)),
+            dma((2, N - 1)),
+            dma((2, N - 1)),
+            dma((2, N)),
+            dma((2, N - 1)),
+            dma((2, N - 1)),
+            dma((2, N - 1)),
+        ],
+        compiler_params=pltpu.CompilerParams(
+            collective_id=0, has_side_effects=True, vmem_limit_bytes=56 * 1024 * 1024
+        ),
+        name="back",
+    )(heads, tokens, gain, wo, wg, wu, wd)
 
 
 def on_device(
@@ -77,7 +429,14 @@
     score_scale = (HD + ROPE) ** (-0.5)
     slot_ids = jnp.arange(per_group, dtype=jnp.int32)
     positions = jnp.arange(capacity, dtype=jnp.int32)
-    results = []
+    tokens = hidden_in.reshape(OWN, WIDTH)
+    tokens_wide = tokens.astype(jnp.float32)
+    partial_latent = jnp.dot(tokens, latent_weight, preferred_element_type=jnp.float32)
+    latent_sum, squared_entry_sum = lax.psum(
+        (partial_latent, jnp.sum(tokens_wide * tokens_wide, axis=1)), "tp"
+    )
+    latents = latent_sum * lax.rsqrt(squared_entry_sum / D + epsilon)[:, None]
+    heads = []
     for step_index in range(STEPS):
         source = source_slots(slot_moves[step_index], groups, per_group)
         held_lengths = lengths[source]
@@ -95,13 +454,7 @@
         own_lengths = lax.dynamic_slice_in_dim(
             held_lengths, group_position_index * per_group, per_group
         )
-        tokens = hidden_in[step_index]
-        tokens_wide = tokens.astype(jnp.float32)
-        partial_latent = jnp.dot(tokens, latent_weight, preferred_element_type=jnp.float32)
-        latent_sum, squared_entry_sum = lax.psum(
-            (partial_latent, jnp.sum(tokens_wide * tokens_wide, axis=1)), "tp"
-        )
-        latent = latent_sum * lax.rsqrt(squared_entry_sum / D + epsilon)[:, None]
+        latent = latents[step_index * per_group : (step_index + 1) * per_group]
         fresh_key = finish_key(latent, own_lengths)
         latent_cache = latent_cache.at[slot_ids, own_lengths].set(fresh_key)
         lengths = held_lengths + 1
@@ -122,40 +475,25 @@
         per_head_latent_vector = jnp.einsum(
             "rht,rtk->rhk", weights, latent_cache[:, :, :KVR], preferred_element_type=jnp.float32
         ).astype(jnp.bfloat16)
-        head_output_rows = jnp.einsum(
-            "gfe,feu->gfu",
-            per_head_latent_vector,
-            value_up_projection,
-            preferred_element_type=jnp.float32,
-        ).astype(jnp.bfloat16)
-        head_output_rows = head_output_rows.reshape(per_group, -1)
-        all_heads = lax.all_gather(head_output_rows, "tp", axis=1, tiled=True)
-        head_block = lax.all_to_all(all_heads, "dp", split_axis=1, concat_axis=0, tiled=True)
-        attention = lax.psum_scatter(
-            jnp.dot(head_block, out_weight, preferred_element_type=jnp.float32),
-            "dp",
-            scatter_dimension=0,
-            tiled=True,
-        )
-        mixed_rows = (tokens_wide + attention).astype(jnp.bfloat16)
-        mixed_all = lax.all_gather(mixed_rows, "dp", axis=0, tiled=True)
-        mixed_wide = mixed_all.astype(jnp.float32)
-        scaled = (mixed_wide * post_gain).astype(jnp.bfloat16)
-        gate_part = jnp.dot(scaled, gate_projection_matrix, preferred_element_type=jnp.float32)
-        up_part = jnp.dot(scaled, up_weight, preferred_element_type=jnp.float32)
-        square_part = jnp.sum(mixed_wide * mixed_wide, axis=1)
-        gate_sum, up_sum, norm_sum = lax.psum((gate_part, up_part, square_part), "tp")
-        activation = activate(gate_sum, up_sum, norm_sum)
-        down_sum = lax.psum_scatter(
-            jnp.dot(activation, down_weight, preferred_element_type=jnp.float32).astype(
-                jnp.bfloat16
-            ),
-            "dp",
-            scatter_dimension=0,
-            tiled=True,
-        ).astype(jnp.float32)
-        results.append((mixed_rows.astype(jnp.float32) + down_sum).astype(jnp.bfloat16))
-    return (jnp.stack(results), latent_cache, lengths)
+        heads.append(
+            jnp.einsum(
+                "gfe,feu->fgu",
+                per_head_latent_vector,
+                value_up_projection,
+                preferred_element_type=jnp.float32,
+            ).astype(jnp.bfloat16)
+        )
+    heads = jnp.concatenate(heads, axis=1).reshape(2 * N, N, OWN, HD)
+    layer_out = back(
+        heads,
+        tokens,
+        post_gain.reshape(1, WIDTH),
+        out_weight,
+        gate_projection_matrix,
+        up_weight,
+        down_weight,
+    )
+    return (layer_out.reshape(STEPS, per_group, WIDTH), latent_cache, lengths)
 
 
 def solution(mesh):

time: 548 us -> 205 us (0.37)
  waiting for transfers between devices: 312 us -> 0.01 us
  Pallas kernels: 0 us -> 99.6 us
  blocking collectives: 109 us -> 14 us
  matrix products: 42.6 us -> 20.4 us
  between operations: 21.6 us -> 8.37 us
  local copies, waits for them, and re-layouts: 29.7 us -> 40 us
  starting transfers between devices: 22.2 us -> 16.1 us
    reduce_scatter x4 -> x0, waiting for transfers between devices: 249 us -> none  [the longest x2 147 us: on_device(): lax.psum_scatter(jnp.dot(activation, down_weight, preferred_element_type=...]
    pallas_call x0 -> x1, Pallas kernels: none -> 99.6 us  [back(): pl.pallas_call(back_kernel, out_shape=jax.ShapeDtypeStruct((OWN, WIDTH),...]
    all_gather x4 -> x0, blocking collectives: 68.5 us -> none  [the longest x2 49.1 us: on_device(): mixed_all = lax.all_gather(mixed_rows, 'dp', axis=0, tiled=True)]
    psum x1 -> x0, waiting for transfers between devices: 52.1 us -> none  [on_device(): lax.psum((gate_part, up_part, square_part), 'tp')]
    dot_general x10 -> x2, matrix products: 25.6 us -> 5.9 us  [on_device(): jnp.einsum('gfe,feu->fgu', per_head_latent_vector, value_up_projection, p...]
    all_to_all x1 -> x0, blocking collectives: 17.7 us -> none  [on_device(): lax.all_to_all(all_heads, 'dp', split_axis=1, concat_axis=0, tiled=True)]
    all_to_all x1 -> x0, starting transfers between devices: 14.3 us -> none  [on_device(): lax.all_to_all(all_heads, 'dp', split_axis=1, concat_axis=0, tiled=True)]
    unnamed x25 -> x16, local copies, waits for them, and re-layouts: 5.05 us -> 14.7 us
  transfers between devices with their start and end apart: 10 -> 4, of which waited for: 7 -> 0; matrix products, arithmetic and copies ran while one was open for 8% -> 17% of each run, Pallas kernels for 0% -> 0%
where the time goes in v1:
time: 205 us; the launch traced here: 203 us
  Pallas kernels  99.6 us (49%)
  local copies, waits for them, and re-layouts  40 us (20%)
  matrix products  20.4 us (10%)
  starting transfers between devices  16.1 us (8%)
  blocking collectives  14 us (7%)
  between operations  8.37 us (4%)
  other arithmetic  4.57 us (2%)
    pallas_call x1, Pallas kernels, back(): pl.pallas_call(back_kernel, out_shape=jax.ShapeDtypeStruct((OWN, WIDTH),...  99.6 us
    ppermute x4, starting transfers between devices, shifted(): return lax.ppermute(block, axis, route)  16.1 us
    unnamed x16, local copies, waits for them, and re-layouts  14.7 us
    psum x1, blocking collectives, on_device(): lax.psum((partial_latent, jnp.sum(tokens_wide * tokens_wide, axis=1)), 'tp')  14 us
    dot_general x2, matrix products, on_device(): jnp.einsum('rhl,rtl->rht', queries[step_index], latent_cache, preferred_e...  7.51 us
    dot_general x2, matrix products, on_device(): jnp.einsum('rht,rtk->rhk', weights, latent_cache[:, :, :KVR], preferred_e...  6.39 us
    dot_general x2, matrix products, on_device(): jnp.einsum('gfe,feu->fgu', per_head_latent_vector, value_up_projection, p...  5.9 us
    squeeze x2, local copies, waits for them, and re-layouts, on_device(): lax.dynamic_index_in_dim(latent_cache, left_out, 0, keepdims=False)  4.52 us
  transfers between devices with their start and end apart: 4, of which 0 were waited for; matrix products, arithmetic and copies ran while one was open for 17% of the time, Pallas kernels for 0%

profile of v1, /device:TPU:1, one launch (start us, length us, event | category | flops | bytes accessed | tf_op | source)
XLA Modules:
  0.0 203.1 jit_solution(14543015244012799630)
XLA Ops:
  0.7 5.0 %copy.37 = bf16[8,448,576]{2,1,0:T(8,128)(2,1)} copy(bf16[8,448,576]{2,1,0:T(8,128)(2,1)} %param.12) | data formatting | bytes 8257536
  10.1 2.4 %dynamic-slice_bitcast_fusion.2 = (bf16[448,576]{1,0:T(8,128)(2,1)}, bf16[448,576]{1,0:T(8,128)(2,1)}) fusion(bf16[8,448,576]{2,1,0:T(8,128)(2,1)} %copy.37, s32[]{:T(128)S(6)} %select_n.76, s32[]{:T(128)S(6)} %select_n.75), kind=kLoop, calls=%fused_computation.32 | loop fusion | bytes 2064392 | tf_op jit(solution)/shard_map/jit(dynamic_index_in_dim)/squeeze | solution.py:449
  12.5 3.0 %collective-permute-start = (bf16[448,576]{1,0:T(8,128)(2,1)}, bf16[448,576]{1,0:T(8,128)(2,1)}, u32[]{:S(2)}, u32[]{:S(2)}) collective-permute-start(bf16[448,576]{1,0:T(8,128)(2,1)} %get-tuple-element.10), channel_id=1, source_target_pairs={{124,0},{0,4},{4,8},{8,12},{12,16},{16,20},{20,24},{24,28},{28,32}... | collective-permute-start | bytes 1548296 | tf_op jit(solution)/shard_map/ppermute | solution.py:31
  18.5 1.9 gather_fusion
  23.5 1.9 gather_fusion.1
  26.3 14.0 %all-reduce = (f32[16,576]{1,0:T(8,128)S(1)}, f32[16]{0:T(128)S(1)}) all-reduce(f32[16,576]{1,0:T(8,128)S(1)} %fusion.49, f32[16]{0:T(128)S(1)} %reduce_sum.48), channel_id=1, replica_groups=mesh['dp'=32,'tp'=4] {'tp'}, use_global_device_ids=true, to_apply=%region_2.0 | all-reduce | flops 9232 | bytes 73856 | tf_op jit(solution)/shard_map/psum | solution.py:435
  44.1 4.1 %copy.17.wg_hbm = bf16[1792,576]{1,0:T(8,128)(2,1)} copy(bf16[1792,576]{0,1:T(8,128)(2,1)} %param.21) | data formatting | bytes 4128768 | tf_op args[9]
  48.2 4.2 %copy.18.wu_hbm = bf16[1792,576]{1,0:T(8,128)(2,1)} copy(bf16[1792,576]{0,1:T(8,128)(2,1)} %param.22) | data formatting | bytes 4128768 | tf_op args[10]
  54.2 1.9 bitcast_dynamic-update-slice_fusion.3
  56.2 1.9 bitcast_dynamic-update-slice_fusion.2
  58.1 2.2 %scatter_fusion.2 = bf16[8,448,576]{2,1,0:T(8,128)(2,1)} fusion(bf16[8,448,576]{2,1,0:T(8,128)(2,1)} %bitcast_dynamic-update-slice_fusion.2, s32[8]{0:T(128)S(1)} %fusion.47, bf16[8,576]{1,0:T(8,128)(2,1)S(1)} %pad_maximum_fusion.1), kind=kCustom, calls=%fused_computation.4 | custom fusion | bytes 27712 | tf_op jit(solution)/shard_map/scatter | solution.py:459
  60.3 1.9 dynamic-slice_bitcast_fusion.1
  62.2 5.1 %collective-permute-start.2 = (bf16[448,576]{1,0:T(8,128)(2,1)}, bf16[448,576]{1,0:T(8,128)(2,1)}, u32[]{:S(2)}, u32[]{:S(2)}) collective-permute-start(bf16[448,576]{1,0:T(8,128)(2,1)} %dynamic-slice_bitcast_fusion.1), channel_id=1, source_target_pairs={{124,0},{0,4},{4,8},{8,12},{12,16},{16,20},{20,24},{24,28},{28,32}... | collective-permute-start | bytes 1548296 | tf_op jit(solution)/shard_map/ppermute | solution.py:31
  67.3 3.8 %fusion.11 = f32[8,32,448]{2,1,0:T(8,128)S(1)} fusion(bf16[8,448,576]{2,1,0:T(8,128)(2,1)} %scatter_fusion.2, bf16[2,8,32,576]{3,2,1,0:T(8,128)(2,1)S(1)} %copy-done.2, pred[8,448]{1,0:T(8,128)(4,1)S(1)} %iota_compare_fusion.1), kind=kOutput, calls=%fused_computation.21 | convolution fusion | flops 132349952 | bytes 4919296 | tf_op jit(solution)/shard_map/rhl,rtl->rht/dot_general | solution.py:463
  71.3 3.6 %fusion.4 = bf16[8,32,512]{2,1,0:T(8,128)(2,1)} fusion(bf16[8,448,576]{2,1,0:T(8,128)(2,1)} %scatter_fusion.2, f32[8,32]{1,0:T(8,128)S(1)} %fusion.54, f32[8,32,448]{2,1,0:T(8,128)S(1)} %fusion.11), kind=kOutput, calls=%fused_computation.12 | convolution fusion | flops 117785280 | bytes 4984832 | tf_op jit(solution)/shard_map/rht,rtk->rhk/dot_general | solution.py:475
  74.8 2.1 %dynamic-slice_bitcast_fusion = (bf16[448,576]{1,0:T(8,128)(2,1)S(1)}, bf16[8,448,576]{2,1,0:T(8,128)(2,1)}) fusion(bf16[8,448,576]{2,1,0:T(8,128)(2,1)} %scatter_fusion.2, s32[]{:T(128)S(6)} %select_n.84, bf16[448,576]{1,0:T(8,128)(2,1)} %collective-permute-done.2), kind=kLoop, calls=%fused_computation.30 | loop fusion | bytes 2236420 | tf_op jit(solution)/shard_map/jit(dynamic_index_in_dim)/squeeze | solution.py:449
  77.0 8.0 %collective-permute-start.3 = (bf16[448,576]{1,0:T(8,128)(2,1)S(1)}, bf16[448,576]{1,0:T(8,128)(2,1)S(1)}, u32[]{:S(2)}, u32[]{:S(2)}) collective-permute-start(bf16[448,576]{1,0:T(8,128)(2,1)S(1)} %get-tuple-element.7), channel_id=1, source_target_pairs={{4,0},{8,4},{12,8},{16,12},{20,16},{24,20},{28,24},{32,28},{36,32}... | collective-permute-start | bytes 1548296 | tf_op jit(solution)/shard_map/ppermute | solution.py:31
  85.5 3.0 %convolution_convert_fusion.1 = bf16[32,8,128]{2,1,0:T(8,128)(2,1)S(1)} fusion(bf16[32,512,128]{2,1,0:T(8,128)(2,1)} %param.18, bf16[8,32,512]{2,1,0:T(8,128)(2,1)} %fusion.4), kind=kOutput, calls=%fused_computation.25 | convolution fusion | flops 33587200 | bytes 4521984 | tf_op jit(solution)/shard_map/gfe,feu->fgu/dot_general | solution.py:479
  89.4 2.2 %scatter_fusion.5 = bf16[8,448,576]{2,1,0:T(8,128)(2,1)} fusion(bf16[8,448,576]{2,1,0:T(8,128)(2,1)} %bitcast_dynamic-update-slice_fusion, s32[8]{0:T(128)S(1)} %fusion.48, bf16[8,576]{1,0:T(8,128)(2,1)S(1)} %pad_maximum_fusion.2), kind=kCustom, calls=%fused_computation.7 | custom fusion | bytes 27712 | tf_op jit(solution)/shard_map/scatter | solution.py:459
  91.6 3.8 %fusion.9 = f32[8,32,448]{2,1,0:T(8,128)S(1)} fusion(bf16[8,448,576]{2,1,0:T(8,128)(2,1)} %scatter_fusion.5, bf16[2,8,32,576]{3,2,1,0:T(8,128)(2,1)S(1)} %copy-done.2, pred[8,448]{1,0:T(8,128)(4,1)S(1)} %iota_compare_fusion), kind=kOutput, calls=%fused_computation.18 | convolution fusion | flops 132349952 | bytes 4919296 | tf_op jit(solution)/shard_map/rhl,rtl->rht/dot_general | solution.py:463
  95.6 2.8 %fusion.2 = bf16[8,32,512]{2,1,0:T(8,128)(2,1)S(1)} fusion(bf16[8,448,576]{2,1,0:T(8,128)(2,1)} %scatter_fusion.5, f32[8,32]{1,0:T(8,128)S(1)} %fusion.53, f32[8,32,448]{2,1,0:T(8,128)S(1)} %fusion.9), kind=kOutput, calls=%fused_computation.10 | convolution fusion | flops 117785280 | bytes 4984832 | tf_op jit(solution)/shard_map/rht,rtk->rhk/dot_general | solution.py:475
  98.4 2.9 %convolution_convert_fusion = bf16[32,8,128]{2,1,0:T(8,128)(2,1)S(1)} fusion(bf16[32,512,128]{2,1,0:T(8,128)(2,1)} %param.18, bf16[8,32,512]{2,1,0:T(8,128)(2,1)S(1)} %fusion.2), kind=kOutput, calls=%fused_computation.24 | convolution fusion | flops 33587200 | bytes 4521984 | tf_op jit(solution)/shard_map/gfe,feu->fgu/dot_general | solution.py:479
  102.0 99.6 %back.1 = bf16[16,1792]{1,0:T(8,128)(2,1)} custom-call(bf16[8,4,16,128]{3,2,1,0:T(8,128)(2,1)} %bitcast.84, bf16[16,1792]{1,0:T(8,128)(2,1)} %bitcast.85, f32[1,1792]{1,0:T(1,128)} %reshape.105.gain, bf16[512,1792]{1,0:T(8,128)(2,1)} %wo_hbm.1, bf16[1792,576]{1,0:T(8,128)(2,1)} %copy.17.wg_hbm, bf16[1792,576]{1,0:T(8,128)(2,1)} %copy.18.wu_hbm, ...), custom_call_target="tpu_custom_call" | custom-call | tf_op jit(solution)/shard_map/back/pallas_call | solution.py:357
  201.7 1.4 copy.38
  (66 shorter events, 11.9 us)
Async XLA Ops:
  0.6 25.0 %copy-start = (bf16[1792,576]{0,1:T(8,128)(2,1)S(1)}, bf16[1792,576]{0,1:T(8,128)(2,1)}, u32[]{:S(2)}) copy-start(bf16[1792,576]{0,1:T(8,128)(2,1)} %param.17) | copy-start | bytes 6193156
  0.6 17.8 %copy-start.1 = (s32[256]{0:T(256)S(1)}, s32[256]{0:T(256)}, u32[]{:S(2)}) copy-start(s32[256]{0:T(256)} %param.13) | copy-start | bytes 3076
  0.7 5.0 %copy-start.5 = (s32[2,32,2]{1,2,0:T(2,128)S(1)}, s32[2,32,2]{1,2,0:T(2,128)}, u32[]{:S(2)}) copy-start(s32[2,32,2]{1,2,0:T(2,128)} %param.14) | copy-start | bytes 1540
  5.7 19.9 %copy-start.3 = (bf16[2,8,1792]{2,1,0:T(8,128)(2,1)S(1)}, bf16[2,8,1792]{2,1,0:T(8,128)(2,1)}, u32[]{:S(2)}) copy-start(bf16[2,8,1792]{2,1,0:T(8,128)(2,1)} %param.15) | copy-start | bytes 172036
  12.5 41.7 %collective-permute-start = (bf16[448,576]{1,0:T(8,128)(2,1)}, bf16[448,576]{1,0:T(8,128)(2,1)}, u32[]{:S(2)}, u32[]{:S(2)}) collective-permute-start(bf16[448,576]{1,0:T(8,128)(2,1)} %get-tuple-element.10), channel_id=1, source_target_pairs={{124,0},{0,4},{4,8},{8,12},{12,16},{16,20},{20,24},{24,28},{28,32}... | collective-permute-start | bytes 1548296 | tf_op jit(solution)/shard_map/ppermute | solution.py:31
  15.6 40.6 %collective-permute-start.1 = (bf16[448,576]{1,0:T(8,128)(2,1)}, bf16[448,576]{1,0:T(8,128)(2,1)}, u32[]{:S(2)}, u32[]{:S(2)}) collective-permute-start(bf16[448,576]{1,0:T(8,128)(2,1)} %get-tuple-element.9), channel_id=1, source_target_pairs={{4,0},{8,4},{12,8},{16,12},{20,16},{24,20},{28,24},{32,28},{36,32}... | collective-permute-start | bytes 1548296 | tf_op jit(solution)/shard_map/ppermute | solution.py:31
  26.3 26.1 %copy-start.4 = (f32[1792]{0:T(1024)S(1)}, f32[1792]{0:T(1024)}, u32[]{:S(2)}) copy-start(f32[1792]{0:T(1024)} %param.20) | copy-start | bytes 21508
  48.2 19.1 %copy-start.2 = (bf16[2,8,32,576]{3,2,1,0:T(8,128)(2,1)S(1)}, bf16[2,8,32,576]{3,2,1,0:T(8,128)(2,1)}, u32[]{:S(2)}) copy-start(bf16[2,8,32,576]{3,2,1,0:T(8,128)(2,1)} %param.16) | copy-start | bytes 1769476
  62.2 12.6 %collective-permute-start.2 = (bf16[448,576]{1,0:T(8,128)(2,1)}, bf16[448,576]{1,0:T(8,128)(2,1)}, u32[]{:S(2)}, u32[]{:S(2)}) collective-permute-start(bf16[448,576]{1,0:T(8,128)(2,1)} %dynamic-slice_bitcast_fusion.1), channel_id=1, source_target_pairs={{124,0},{0,4},{4,8},{8,12},{12,16},{16,20},{20,24},{24,28},{28,32}... | collective-permute-start | bytes 1548296 | tf_op jit(solution)/shard_map/ppermute | solution.py:31
  77.0 11.6 %collective-permute-start.3 = (bf16[448,576]{1,0:T(8,128)(2,1)S(1)}, bf16[448,576]{1,0:T(8,128)(2,1)S(1)}, u32[]{:S(2)}, u32[]{:S(2)}) collective-permute-start(bf16[448,576]{1,0:T(8,128)(2,1)S(1)} %get-tuple-element.7), channel_id=1, source_target_pairs={{4,0},{8,4},{12,8},{16,12},{20,16},{24,20},{28,24},{32,28},{36,32}... | collective-permute-start | bytes 1548296 | tf_op jit(solution)/shard_map/ppermute | solution.py:31

commit v2 on v0

v2 whole, which is shorter than its diff:
```python
import math
import types

import jax
import jax.numpy as jnp
from jax import lax
from jax.experimental import pallas as pl
from jax.experimental.pallas import tpu as pltpu
from jax.sharding import PartitionSpec as P

D = 7168
KVR = 512
ROPE = 64
HD = 128
STEPS = 2
ROWS_DEV = 8
N = 4
OWN = STEPS * ROWS_DEV
BLOCKS = N * N
HALF = BLOCKS * ROWS_DEV
WIDTH = D // N
COLS = WIDTH // 2
TILE = 2 * ROWS_DEV
FF_DEV = 576
CHUNK = 2 * HALF // N
HEADS = 32
LAT = KVR + ROPE
GROUPS = 2 * N * N
EARLY = 4
NEAR_FIRST = (1, 3, 2)
FAR_FIRST = (2, 1, 3)
MESH = pl.DeviceIdType.MESH


epsilon = 1e-06


def dot_rows(lhs, rhs):
    return lax.dot_general(
        lhs, rhs, (((1,), (1,)), ((), ())), preferred_element_type=jnp.float32
    )


class Place:
    def __init__(self):
        dp = lax.axis_index("dp")
        self.x = lax.axis_index("tp")
        self.y = dp // (2 * N)
        self.z = (dp // 2) % N
        self.c = dp % 2
        self.first = self.c * self.y + (1 - self.c) * self.z
        self.second = self.c * self.z + (1 - self.c) * self.y
        self.me = dp

    def group(self, y, z, c):
        return y * (2 * N) + z * 2 + c

    def on_first(self, k):
        y = self.c * k + (1 - self.c) * self.y
        z = self.c * self.z + (1 - self.c) * k
        return {"dp": self.group(y, z, self.c), "tp": self.x}

    def on_second(self, k):
        y = self.c * self.y + (1 - self.c) * k
        z = self.c * k + (1 - self.c) * self.z
        return {"dp": self.group(y, z, self.c), "tp": self.x}

    def on_core(self):
        return {"dp": self.group(self.y, self.z, 1 - self.c), "tp": self.x}

    def on_x(self, k):
        return {"dp": self.me, "tp": k}

    def on_ring(self, o):
        return {"dp": lax.rem(self.me + o + GROUPS, GROUPS), "tp": self.x}


def remote(src, dst, send_sem, recv_sem, device):
    return pltpu.make_async_remote_copy(
        src_ref=src,
        dst_ref=dst,
        send_sem=send_sem,
        recv_sem=recv_sem,
        device_id=device,
        device_id_type=MESH,
    )


def send(*args):
    copy = remote(*args)
    copy.start()
    return copy


def stacked(rows):
    left = rows[:, :COLS].reshape(-1, ROWS_DEV, COLS)
    right = rows[:, COLS:].reshape(-1, ROWS_DEV, COLS)
    return jnp.concatenate([left, right], axis=1)


def unstacked(blocks):
    left = blocks[:, :ROWS_DEV].reshape(-1, COLS)
    right = blocks[:, ROWS_DEV:].reshape(-1, COLS)
    return jnp.concatenate([left, right], axis=1)


def project(lhs, weight, out):
    for start in range(0, COLS, 256):
        width = min(256, COLS - start)
        parts = [
            jnp.dot(
                lhs, weight[:, first + start : first + start + width], preferred_element_type=jnp.float32
            ).reshape(-1, ROWS_DEV, width)
            for first in (0, COLS)
        ]
        out[:, :, start : start + width] = jnp.concatenate(parts, axis=1).astype(jnp.bfloat16)


def source_of(moves, step, group, slot):
    right = lax.rem(group + 1, GROUPS)
    left = lax.rem(group + GROUPS - 1, GROUPS)
    to_right = slot == moves[step, 0, group]
    to_left = slot == moves[step, 1, group]
    source_group = jnp.where(to_right, right, jnp.where(to_left, left, group))
    source_slot = jnp.where(
        to_right, moves[step, 1, right], jnp.where(to_left, moves[step, 0, left], slot)
    )
    return source_group, source_slot


def held_first(lengths, moves, group, slot):
    source_group, source_slot = source_of(moves, 0, group, slot)
    return lengths[source_group * ROWS_DEV + source_slot]


def held_second(lengths, moves, group, slot):
    source_group, source_slot = source_of(moves, 1, group, slot)
    return held_first(lengths, moves, source_group, source_slot) + 1


def slot_order(moves, group):
    free_before, slots, places = 0, [0] * ROWS_DEV, []
    for j in range(ROWS_DEV):
        moved = (
            (j == moves[0, 0, group])
            | (j == moves[0, 1, group])
            | (j == moves[1, 0, group])
            | (j == moves[1, 1, group])
        )
        early = jnp.where(moved | (free_before >= EARLY), 0, 1)
        place = jnp.where(early == 1, free_before, EARLY + j - free_before)
        places.append(place)
        slots = [jnp.where(place == p, j, slots[p]) for p in range(ROWS_DEV)]
        free_before = free_before + early
    return slots, places


def with_row(block, position, row):
    rows = lax.broadcasted_iota(jnp.int32, block.shape, 0)
    return jnp.where(rows == position, jnp.broadcast_to(row, block.shape), block)


def attend(query_rows, keys, live):
    scores = dot_rows(query_rows, keys[...]) * (HD + ROPE) ** (-0.5)
    positions = lax.broadcasted_iota(jnp.int32, scores.shape, 1)
    scores = jnp.where(positions < live, scores, -1e30)
    powers = jnp.exp(scores - jnp.max(scores, axis=1, keepdims=True))
    weights = (powers / jnp.sum(powers, axis=1, keepdims=True)).astype(jnp.bfloat16)
    return jnp.dot(weights, keys[:, :KVR], preferred_element_type=jnp.float32)


def fresh_keys(latent, positions):
    content = latent[:, :KVR]
    content = content * lax.rsqrt(jnp.mean(content * content, axis=1, keepdims=True) + epsilon)
    rotary = latent[:, KVR:]
    lane = lax.broadcasted_iota(jnp.int32, rotary.shape, 1)
    half = ROPE // 2
    power = lax.rem(lane, half).astype(jnp.float32) * (-2.0 / ROPE * math.log(10000.0))
    angles = positions.astype(jnp.float32) * jnp.exp(power)
    turned = jnp.where(lane < half, -pltpu.roll(rotary, 128 - half, 1), pltpu.roll(rotary, half, 1))
    return content, rotary * jnp.cos(angles) + turned * jnp.sin(angles)


def enter(here, barrier):
    devices = [here.on_ring(1), here.on_ring(-1), here.on_core()]
    for o in range(1, N):
        devices.append(here.on_x(lax.rem(here.x + o, N)))
        devices.append(here.on_first(lax.rem(here.first + o, N)))
        devices.append(here.on_second(lax.rem(here.second + o, N)))
    for device in devices:
        pl.semaphore_signal(barrier, inc=1, device_id=device, device_id_type=MESH)

    @pl.loop(0, GROUPS)
    def _(i):
        d = lax.rem(here.me + i, GROUPS)

        @pl.when((d != here.me) | (here.x != here.y))
        def _():
            pl.semaphore_signal(barrier, inc=1, device_id={"dp": d, "tp": here.y}, device_id_type=MESH)

    return len(devices) + GROUPS - 1 + jnp.where(here.x == here.y, 0, 1)


def head_copy(here, r, step, i):
    place = here.c * BLOCKS + here.first * N + here.second
    k = lax.rem(here.z * 2 + here.c + i // N, 2 * N)
    x = lax.rem(here.x + i, N)
    kept = (x == here.x) & (here.x * (2 * N) + k == here.me)

    def copy():
        return remote(
            r.heads.at[step, k],
            r.head_rows.at[step, place],
            r.head_send.at[step, i],
            r.head_recv.at[step, place],
            {"dp": here.x * (2 * N) + k, "tp": x},
        )

    def local():
        return pltpu.make_async_copy(
            r.heads.at[step, k], r.head_rows.at[step, place], r.head_recv.at[step, place]
        )

    return kept, copy, local


def value_up(here, r, step, places):
    for j in range(ROWS_DEV):
        block = r.head_latent[step * ROWS_DEV + places[j]]
        for c in range(KVR // 128):
            r.head_sorted[c, j * HEADS : (j + 1) * HEADS, :] = block[:, c * 128 : (c + 1) * 128]

    def head(h):
        rows = jnp.concatenate(
            [r.head_sorted.at[c][pl.ds(h, ROWS_DEV, stride=HEADS), :] for c in range(KVR // 128)], axis=1
        ).astype(jnp.bfloat16)
        return jnp.dot(rows, r.vup[h], preferred_element_type=jnp.float32)

    for h in range(0, HEADS, 2):
        r.heads[step, h // N, h % N // 2] = jnp.concatenate([head(h), head(h + 1)], axis=0).astype(jnp.bfloat16)

    @pl.loop(0, GROUPS)
    def _(i):
        kept, copy, local = head_copy(here, r, step, i)

        @pl.when(kept)
        def _():
            local().start()

        @pl.when(jnp.logical_not(kept))
        def _():
            copy().start()


def front_line(here, r):
    loads = []
    for i, (src, dst) in enumerate(
        (
            (r.cache_hbm, r.cache),
            (r.lw_hbm, r.lw),
            (r.queries_hbm, r.queries),
            (r.vup_hbm, r.vup),
            (r.wo_hbm, r.wo),
            (r.wg_hbm, r.wg),
            (r.wu_hbm, r.wu),
            (r.wd_hbm, r.wd),
        )
    ):
        load = pltpu.make_async_copy(src, dst, r.load_sem.at[i])
        load.start()
        loads.append(load)
    r.weight_loads = loads[4:]
    barrier = pltpu.get_barrier_semaphore()
    entered = enter(here, barrier)

    moves, me = r.moves, here.me
    a0, b0, a1, b1 = moves[0, 0, me], moves[0, 1, me], moves[1, 0, me], moves[1, 1, me]
    slots, places = slot_order(moves, me)

    loads[0].wait()
    r.leaving0[0] = r.cache[a0]
    r.leaving0[1] = r.cache[b0]
    pl.semaphore_wait(barrier, entered)
    moving0 = [
        send(r.leaving0.at[i], r.arrived0.at[i], r.move0_sem.at[0, i], r.move0_sem.at[1, i], here.on_ring(o))
        for i, o in enumerate((1, -1))
    ]

    loads[1].wait()
    wide = r.tokens[...].astype(jnp.float32)
    r.latents[...] = jnp.zeros_like(r.latents)
    r.latents[:, :LAT] = dot_rows(r.tokens[...], r.lw[...])
    r.latents[:, LAT + 64 :] = jnp.broadcast_to(jnp.sum(wide * wide, axis=1, keepdims=True), (OWN, 128))
    copies = [
        send(
            r.latents,
            r.latent_rows.at[o - 1],
            r.latent_sem.at[0, o - 1],
            r.latent_sem.at[1, o - 1],
            here.on_x(lax.rem(here.x + o, N)),
        )
        for o in FAR_FIRST
    ]
    held = [held_first(r.lengths, moves, me, j) for j in range(ROWS_DEV)]
    held += [held_second(r.lengths, moves, me, j) for j in range(ROWS_DEV)]
    row = lax.broadcasted_iota(jnp.int32, (OWN, 128), 0)
    positions = jnp.zeros((OWN, 128), jnp.int32)
    for i in range(OWN):
        positions = jnp.where(row == i, held[i], positions)

    def held_at(step, place):
        result = held[step * ROWS_DEV]
        for j in range(1, ROWS_DEV):
            result = jnp.where(slots[place] == j, held[step * ROWS_DEV + j], result)
        return result

    yield
    for copy in copies:
        copy.wait()
    total = r.latents[...]
    for o in range(N - 1):
        total = total + r.latent_rows[o]
    scale = lax.rsqrt(total[:, LAT + 64 :] / D + epsilon)[:, :1]
    content, rotary = fresh_keys(total[:, : LAT + 64] * scale, positions)
    r.fresh[:, :KVR] = content
    r.fresh[:, KVR:] = rotary

    def fresh_row(step, place):
        return r.fresh[pl.ds(step * ROWS_DEV + slots[place], 1), :LAT].astype(jnp.bfloat16)

    loads[2].wait()
    r.ordered_copies = []
    for p in range(EARLY):
        first, second = held_at(0, p), held_at(1, p)
        block = with_row(r.cache[slots[p]], first, fresh_row(0, p))
        r.early_keys[p] = with_row(block, second, fresh_row(1, p))
        copy = pltpu.make_async_copy(r.early_keys.at[p], r.ordered.at[p], r.out_sem.at[p])
        copy.start()
        r.ordered_copies.append(copy)
        rows = jnp.concatenate([r.queries[0, slots[p]], r.queries[1, slots[p]]], axis=0)
        step_row = lax.broadcasted_iota(jnp.int32, (2 * HEADS, 1), 0)
        live = jnp.where(step_row < HEADS, first + 1, second + 1)
        result = attend(rows, r.early_keys.at[p], live)
        r.head_latent[p] = result[:HEADS]
        r.head_latent[ROWS_DEV + p] = result[HEADS:]

    yield
    for copy in moving0:
        copy.wait()
    for p in range(EARLY, ROWS_DEV):
        block = jnp.where(
            slots[p] == a0, r.arrived0[1], jnp.where(slots[p] == b0, r.arrived0[0], r.cache[slots[p]])
        )
        r.keys0[p - EARLY] = with_row(block, held_at(0, p), fresh_row(0, p))
    place_a, place_b = 0, 0
    for p in range(EARLY, ROWS_DEV):
        place_a = jnp.where(slots[p] == a1, p - EARLY, place_a)
        place_b = jnp.where(slots[p] == b1, p - EARLY, place_b)
    r.leaving1[0] = r.keys0[place_a]
    r.leaving1[1] = r.keys0[place_b]
    moving1 = [
        send(r.leaving1.at[i], r.arrived1.at[i], r.move1_sem.at[0, i], r.move1_sem.at[1, i], here.on_ring(o))
        for i, o in enumerate((1, -1))
    ]
    for p in range(EARLY, ROWS_DEV):
        r.head_latent[p] = attend(r.queries[0, slots[p]], r.keys0.at[p - EARLY], held_at(0, p) + 1)
    loads[3].wait()
    value_up(here, r, 0, places)

    yield
    for copy in moving1:
        copy.wait()
    for p in range(EARLY, ROWS_DEV):
        block = jnp.where(
            slots[p] == a1, r.arrived1[1], jnp.where(slots[p] == b1, r.arrived1[0], r.keys0[p - EARLY])
        )
        r.keys1[p - EARLY] = with_row(block, held_at(1, p), fresh_row(1, p))
        copy = pltpu.make_async_copy(r.keys1.at[p - EARLY], r.ordered.at[p], r.out_sem.at[p])
        copy.start()
        r.ordered_copies.append(copy)
    for p in range(EARLY, ROWS_DEV):
        r.head_latent[ROWS_DEV + p] = attend(
            r.queries[1, slots[p]], r.keys1.at[p - EARLY], held_at(1, p) + 1
        )
    yield
    value_up(here, r, 1, places)
    yield


def reduce_over_groups(here, r, step, use):
    own, peer = r.own.at[step], r.peer_rows.at[use, step]
    core_sem, sem1, sem2 = r.core_sem.at[use, step], r.sem1.at[use, step], r.sem2.at[use, step]
    sums, parts, rows1, rows2 = r.sums.at[step], r.parts.at[step], r.rows1.at[use, step], r.rows2.at[use, step]
    remote(r.to_peer.at[step], peer, core_sem.at[0], core_sem.at[1], here.on_core()).wait()

    def both(k):
        blocks = pl.ds(k * N, N)
        return own[blocks].astype(jnp.float32) + peer[blocks].astype(jnp.float32)

    copies = {}
    for o in FAR_FIRST:
        k = lax.rem(here.first + o, N)
        sums[k] = both(k).astype(jnp.bfloat16)
        copies[o] = send(sums.at[k], rows1.at[o - 1], sem1.at[0, o - 1], sem1.at[1, o - 1], here.on_first(k))
    total = both(here.first)
    yield
    for o in NEAR_FIRST:
        copies[o].wait()
        total = total + rows1[o - 1].astype(jnp.float32)
    parts[...] = total.astype(jnp.bfloat16)
    copies = {}
    for o in FAR_FIRST:
        k = lax.rem(here.second + o, N)
        copies[o] = send(parts.at[k], rows2.at[o - 1], sem2.at[0, o - 1], sem2.at[1, o - 1], here.on_second(k))
    yield
    total = parts[here.second].astype(jnp.float32)
    for o in NEAR_FIRST:
        copies[o].wait()
        total = total + rows2[o - 1].astype(jnp.float32)
    return total


def project_both(here, r, step, use, lhs, weight):
    project(lhs(1 - here.c), weight, r.to_peer.at[step])
    core_sem = r.core_sem.at[use, step]
    send(r.to_peer.at[step], r.peer_rows.at[use, step], core_sem.at[0], core_sem.at[1], here.on_core())
    project(lhs(here.c), weight, r.own.at[step])


def back_line(here, r, step):
    f32, bf16 = jnp.float32, jnp.bfloat16

    @pl.loop(0, GROUPS)
    def _(i):
        pltpu.make_async_copy(r.heads.at[step, 0], r.head_rows.at[step, i], r.head_recv.at[step, i]).wait()

    @pl.loop(0, GROUPS)
    def _(i):
        kept, copy, _ = head_copy(here, r, step, i)

        @pl.when(jnp.logical_not(kept))
        def _():
            copy().wait_send()

    rows = r.head_rows[step].astype(f32)
    for h in range(N):
        first = h % 2 * ROWS_DEV
        r.head_block[:, h * HD : (h + 1) * HD] = (
            rows[:, h // 2, first : first + ROWS_DEV].reshape(2 * HALF, HD).astype(bf16)
        )
    if step == 0:
        r.weight_loads[0].wait()

    def half(ref, c):
        return ref[pl.ds(pl.multiple_of(c * HALF, HALF), HALF), :]

    project_both(here, r, step, 0, lambda c: half(r.head_block, c), r.wo[...])
    yield
    attention = yield from reduce_over_groups(here, r, step, 0)
    tokens = stacked(r.tokens[...].astype(f32)[step * ROWS_DEV : (step + 1) * ROWS_DEV])[0]
    mixed = (tokens + attention).astype(bf16).astype(f32)
    r.mixed[step] = mixed

    squares = jnp.sum(mixed * mixed, axis=1, keepdims=True)
    squares = squares[:ROWS_DEV] + squares[ROWS_DEV:]
    norms, norm_rows, sem = r.norms.at[step], r.norm_rows.at[step], r.norm_sem.at[step]
    norms[...] = jnp.broadcast_to(squares, norms.shape)
    copies = {}
    for o in FAR_FIRST:
        x = lax.rem(here.x + o, N)
        copies[o] = send(norms, norm_rows.at[o - 1], sem.at[0, o - 1], sem.at[1, o - 1], here.on_x(x))
    yield
    squares = norms[...]
    for o in NEAR_FIRST:
        copies[o].wait()
        squares = squares + norm_rows[o - 1]
    scale = lax.rsqrt(squares / D + epsilon)[:, :1]
    scale = jnp.concatenate([scale, scale], axis=0)
    gain = stacked(jnp.broadcast_to(r.gain[...].reshape(1, WIDTH), (ROWS_DEV, WIDTH)))[0]
    mixed_all = r.mixed_all.at[step]
    mixed_all[here.c, here.first, here.second] = (r.mixed[step] * gain * scale).astype(bf16)

    mine = mixed_all.at[here.c, here.first, here.second]
    sem = r.gather2.at[step]
    copies = {}
    for o in FAR_FIRST:
        k = lax.rem(here.second + o, N)
        copies[o] = send(mine, mine, sem.at[0, o - 1], sem.at[1, o - 1], here.on_second(k))
    yield
    for o in NEAR_FIRST:
        copies[o].wait()
    mine = mixed_all.at[here.c, here.first]
    sem, core_sem = r.gather1.at[step], r.gather_core.at[step]
    copies = {}
    for o in FAR_FIRST:
        k = lax.rem(here.first + o, N)
        copies[o] = send(mine, mine, sem.at[0, o - 1], sem.at[1, o - 1], here.on_first(k))
    handed = [send(mine, mine, core_sem.at[0, 0], core_sem.at[1, 0], here.on_core())]
    yield
    for o in NEAR_FIRST:
        copies[o].wait()
        block = mixed_all.at[here.c, lax.rem(here.first + N - o, N)]
        handed.append(send(block, block, core_sem.at[0, o], core_sem.at[1, o], here.on_core()))

    if step == 0:
        r.weight_loads[1].wait()
        r.weight_loads[2].wait()
    sums = (
        (r.gate_part.at[step], r.gate_rows.at[step], r.gate_sem.at[step], r.wg),
        (r.up_part.at[step], r.up_rows.at[step], r.up_sem.at[step], r.wu),
    )

    def chunk_copy(part, rows, sem, k):
        slot = lax.rem(k - here.x + N, N) - 1
        return remote(part.at[k], rows.at[slot], sem.at[0, slot], sem.at[1, slot], here.on_x(k))

    for core in (here.c, 1 - here.c):
        if core is not here.c:
            yield
            for copy in handed:
                copy.wait()
        r.lhs[...] = unstacked(mixed_all[core].astype(f32).reshape(BLOCKS, TILE, COLS)).astype(bf16)
        for part, rows, sem, weight in sums:
            part[pl.ds(2 * core, 2)] = dot_rows(r.lhs[...], weight[...]).astype(bf16).reshape(2, CHUNK, FF_DEV)
            for i in range(2):
                k = 2 * core + lax.rem(here.x + i, 2)

                @pl.when(k != here.x)
                def _():
                    chunk_copy(part, rows, sem, k).start()

    yield
    totals = []
    for part, rows, sem, _ in sums:
        total = part[here.x].astype(f32)
        for o in NEAR_FIRST:
            chunk_copy(part, rows, sem, lax.rem(here.x + o, N)).wait()
        for o in range(N - 1):
            total = total + rows[o].astype(f32)
        totals.append(total)
    gate, up = totals
    activation = r.activation.at[step]
    activation[here.x] = (gate / (1.0 + jnp.exp(-gate)) * up).astype(bf16)
    mine = activation.at[here.x]
    sem = r.act_sem.at[step]
    copies = {}
    for o in FAR_FIRST:
        x = lax.rem(here.x + o, N)
        copies[o] = send(mine, mine, sem.at[0, o - 1], sem.at[1, o - 1], here.on_x(x))
    yield
    for o in NEAR_FIRST:
        copies[o].wait()

    if step == 0:
        r.weight_loads[3].wait()
    project_both(
        here, r, step, 1, lambda c: activation[pl.ds(2 * c, 2)].reshape(HALF, FF_DEV), r.wd[...]
    )
    yield
    down = yield from reduce_over_groups(here, r, step, 1)
    r.results[step] = unstacked((r.mixed[step] + down)[None])
    yield


ORDER = "FFFF0F001010101010101010101010111"

INPUTS = (
    "lengths", "moves", "tokens", "gain", "lw_hbm", "queries_hbm", "cache_hbm", "vup_hbm",
    "wo_hbm", "wg_hbm", "wu_hbm", "wd_hbm",
)


def layer_kernel(names, *refs):
    r = types.SimpleNamespace(**dict(zip(names, refs)))
    here = Place()
    lines = {"F": front_line(here, r), "0": back_line(here, r, 0), "1": back_line(here, r, 1)}
    for name in ORDER:
        next(lines[name], None)
    r.out[...] = jnp.concatenate([r.results[0], r.results[1]], axis=0).astype(jnp.bfloat16)
    for copy in r.ordered_copies:
        copy.wait()


def layer(lengths, moves, tokens, gain, lw, queries, cache, vup, wo, wg, wu, wd):
    bf16, f32 = jnp.bfloat16, jnp.float32
    vmem = pl.BlockSpec(memory_space=pltpu.VMEM)
    smem = pl.BlockSpec(memory_space=pltpu.SMEM)
    hbm = pl.BlockSpec(memory_space=pl.ANY)
    slot = cache.shape[1:]

    def dma(*shape):
        return pltpu.SemaphoreType.DMA(shape)

    def held(*shape, dtype=bf16):
        return pltpu.VMEM(shape, dtype)

    scratch = dict(
        cache=held(*cache.shape),
        lw=held(*lw.shape),
        queries=held(*queries.shape),
        vup=held(*vup.shape),
        wo=held(*wo.shape),
        wg=held(*wg.shape),
        wu=held(*wu.shape),
        wd=held(*wd.shape),
        latents=held(OWN, LAT + 64 + 128, dtype=f32),
        latent_rows=held(N - 1, OWN, LAT + 64 + 128, dtype=f32),
        fresh=held(OWN, LAT + 64, dtype=f32),
        leaving0=held(2, *slot),
        leaving1=held(2, *slot),
        arrived0=held(2, *slot),
        arrived1=held(2, *slot),
        early_keys=held(EARLY, *slot),
        keys0=held(ROWS_DEV - EARLY, *slot),
        keys1=held(ROWS_DEV - EARLY, *slot),
        head_latent=held(OWN, HEADS, KVR, dtype=f32),
        head_sorted=held(KVR // 128, ROWS_DEV * HEADS, 128, dtype=f32),
        heads=held(STEPS, 2 * N, N // 2, TILE, HD),
        head_rows=held(STEPS, GROUPS, N // 2, TILE, HD),
        head_block=held(2 * HALF, N * HD),
        to_peer=held(STEPS, BLOCKS, TILE, COLS),
        own=held(STEPS, BLOCKS, TILE, COLS),
        peer_rows=held(2, STEPS, BLOCKS, TILE, COLS),
        sums=held(STEPS, N, N, TILE, COLS),
        parts=held(STEPS, N, TILE, COLS),
        rows1=held(2, STEPS, N - 1, N, TILE, COLS),
        rows2=held(2, STEPS, N - 1, TILE, COLS),
        mixed=held(STEPS, TILE, COLS, dtype=f32),
        norms=held(STEPS, ROWS_DEV, 128, dtype=f32),
        norm_rows=held(STEPS, N - 1, ROWS_DEV, 128, dtype=f32),
        mixed_all=held(STEPS, 2, N, N, TILE, COLS),
        lhs=held(HALF, WIDTH),
        gate_part=held(STEPS, N, CHUNK, FF_DEV),
        up_part=held(STEPS, N, CHUNK, FF_DEV),
        gate_rows=held(STEPS, N - 1, CHUNK, FF_DEV),
        up_rows=held(STEPS, N - 1, CHUNK, FF_DEV),
        activation=held(STEPS, N, CHUNK, FF_DEV),
        results=held(STEPS, ROWS_DEV, WIDTH, dtype=f32),
        load_sem=dma(8),
        latent_sem=dma(2, N - 1),
        move0_sem=dma(2, 2),
        move1_sem=dma(2, 2),
        out_sem=dma(ROWS_DEV),
        head_send=dma(STEPS, GROUPS),
        head_recv=dma(STEPS, GROUPS),
        core_sem=dma(2, STEPS, 2),
        sem1=dma(2, STEPS, 2, N - 1),
        sem2=dma(2, STEPS, 2, N - 1),
        norm_sem=dma(STEPS, 2, N - 1),
        gather2=dma(STEPS, 2, N - 1),
        gather1=dma(STEPS, 2, N - 1),
        gather_core=dma(STEPS, 2, N),
        gate_sem=dma(STEPS, 2, N - 1),
        up_sem=dma(STEPS, 2, N - 1),
        act_sem=dma(STEPS, 2, N - 1),
    )
    names = (*INPUTS, "out", "ordered", *scratch)

    def kernel(*refs):
        layer_kernel(names, *refs)

    return pl.pallas_call(
        kernel,
        out_shape=(
            jax.ShapeDtypeStruct((OWN, WIDTH), bf16),
            jax.ShapeDtypeStruct(cache.shape, bf16),
        ),
        in_specs=[smem, smem, vmem, vmem] + [hbm] * 8,
        out_specs=(vmem, hbm),
        scratch_shapes=list(scratch.values()),
        compiler_params=pltpu.CompilerParams(
            collective_id=0, has_side_effects=True, vmem_limit_bytes=58 * 1024 * 1024
        ),
        name="layer",
    )(lengths, moves, tokens, gain, lw, queries, cache, vup, wo, wg, wu, wd)


def finish_kernel(
    lengths, moves, group, ordered, rows, final_cache, final_rows, final_lengths, moved, slots, row_block, sems, row_sem
):
    _, places = slot_order(moves, group[0])
    loads = [pltpu.make_async_copy(ordered.at[places[j]], slots.at[j], sems.at[0, j]) for j in range(ROWS_DEV)]
    stores = [pltpu.make_async_copy(slots.at[j], final_cache.at[j], sems.at[1, j]) for j in range(ROWS_DEV)]
    loads.append(pltpu.make_async_copy(rows, row_block, row_sem.at[0]))
    stores.append(pltpu.make_async_copy(row_block, final_rows, row_sem.at[1]))
    for load in loads:
        load.start()
    for load, store in zip(loads, stores):
        load.wait()
        store.start()

    @pl.loop(0, GROUPS)
    def _(g):
        for j in range(ROWS_DEV):
            moved[g * ROWS_DEV + j] = lengths[g * ROWS_DEV + j] + 1

    @pl.loop(0, GROUPS)
    def _(g):
        right = lax.rem(g + 1, GROUPS)
        left = lax.rem(g + GROUPS - 1, GROUPS)
        moved[g * ROWS_DEV + moves[0, 0, g]] = lengths[right * ROWS_DEV + moves[0, 1, right]] + 1
        moved[g * ROWS_DEV + moves[0, 1, g]] = lengths[left * ROWS_DEV + moves[0, 0, left]] + 1

    @pl.loop(0, GROUPS)
    def _(g):
        for j in range(ROWS_DEV):
            final_lengths[g * ROWS_DEV + j] = moved[g * ROWS_DEV + j] + 1

    @pl.loop(0, GROUPS)
    def _(g):
        right = lax.rem(g + 1, GROUPS)
        left = lax.rem(g + GROUPS - 1, GROUPS)
        final_lengths[g * ROWS_DEV + moves[1, 0, g]] = moved[right * ROWS_DEV + moves[1, 1, right]] + 1
        final_lengths[g * ROWS_DEV + moves[1, 1, g]] = moved[left * ROWS_DEV + moves[1, 0, left]] + 1

    for store in stores:
        store.wait()


def finish(lengths, moves, group, ordered, rows):
    smem = pl.BlockSpec(memory_space=pltpu.SMEM)
    hbm = pl.BlockSpec(memory_space=pltpu.HBM)
    return pl.pallas_call(
        finish_kernel,
        out_shape=(
            jax.ShapeDtypeStruct(ordered.shape, ordered.dtype),
            jax.ShapeDtypeStruct(rows.shape, rows.dtype),
            jax.ShapeDtypeStruct(lengths.shape, jnp.int32),
        ),
        in_specs=[smem, smem, smem, hbm, hbm],
        out_specs=(hbm, hbm, smem),
        scratch_shapes=[
            pltpu.SMEM(lengths.shape, jnp.int32),
            pltpu.VMEM(ordered.shape, ordered.dtype),
            pltpu.VMEM(rows.shape, rows.dtype),
            pltpu.SemaphoreType.DMA((2, ROWS_DEV)),
            pltpu.SemaphoreType.DMA((2,)),
        ],
        compiler_params=pltpu.CompilerParams(vmem_limit_bytes=16 * 1024 * 1024),
        name="finish",
    )(lengths, moves, group, ordered, rows)


def on_device(
    latent_cache,
    lengths,
    slot_moves,
    hidden_in,
    queries,
    latent_weight,
    value_up_projection,
    out_weight,
    post_gain,
    gate_projection_matrix,
    up_weight,
    down_weight,
):
    moves = jnp.swapaxes(slot_moves, 1, 2)
    rows, ordered = layer(
        lengths,
        moves,
        hidden_in.reshape(OWN, WIDTH),
        post_gain,
        latent_weight.T,
        queries,
        latent_cache,
        value_up_projection,
        out_weight,
        gate_projection_matrix.T,
        up_weight.T,
        down_weight,
    )
    group = lax.axis_index("dp").reshape(1)
    final_cache, final_rows, final_lengths = finish(lengths, moves, group, ordered, rows)
    return (final_rows.reshape(STEPS, ROWS_DEV, WIDTH), final_cache, final_lengths)


def solution(mesh):
    return jax.shard_map(
        on_device,
        mesh=mesh,
        in_specs=(
            P("dp", None, None),
            P(),
            P(),
            P(None, "dp", "tp"),
            P(None, "dp", "tp", None),
            P("tp", None),
            P("tp", None, None),
            P("dp", "tp"),
            P("tp"),
            P("tp", "dp"),
            P("tp", "dp"),
            P("dp", "tp"),
        ),
        out_specs=(P(None, "dp", "tp"), P("dp", None, None), P()),
        check_vma=False,
    )
```

time: 548 us -> 114 us (0.21)
  waiting for transfers between devices: 312 us -> 0 us
  Pallas kernels: 0 us -> 110 us
  blocking collectives: 109 us -> 0 us
  matrix products: 42.6 us -> 0 us
  local copies, waits for them, and re-layouts: 29.7 us -> 3.12 us
  starting transfers between devices: 22.2 us -> 0 us
  between operations: 21.6 us -> 0.85 us
  other arithmetic: 8.83 us -> 0 us
    reduce_scatter x4 -> x0, waiting for transfers between devices: 249 us -> none  [the longest x2 147 us: on_device(): lax.psum_scatter(jnp.dot(activation, down_weight, preferred_element_type=...]
    pallas_call x0 -> x2, Pallas kernels: none -> 110 us  [the longest x1 105 us: layer(): pl.pallas_call(kernel, out_shape=(jax.ShapeDtypeStruct((OWN, WIDTH), bf16...]
    all_gather x4 -> x0, blocking collectives: 68.5 us -> none  [the longest x2 49.1 us: on_device(): mixed_all = lax.all_gather(mixed_rows, 'dp', axis=0, tiled=True)]
    psum x1 -> x0, waiting for transfers between devices: 52.1 us -> none  [on_device(): lax.psum((gate_part, up_part, square_part), 'tp')]
    dot_general x16 -> x0, matrix products: 42.6 us -> none  [the longest x2 7.6 us: on_device(): jnp.einsum('rhl,rtl->rht', queries[step_index], latent_cache, preferred_e...]
    psum x2 -> x0, blocking collectives: 22.4 us -> none  [the longest x1 14 us: on_device(): lax.psum((partial_latent, jnp.sum(tokens_wide * tokens_wide, axis=1)), 'tp')]
    all_to_all x1 -> x0, blocking collectives: 17.7 us -> none  [on_device(): lax.all_to_all(all_heads, 'dp', split_axis=1, concat_axis=0, tiled=True)]
    all_to_all x1 -> x0, starting transfers between devices: 14.3 us -> none  [on_device(): lax.all_to_all(all_heads, 'dp', split_axis=1, concat_axis=0, tiled=True)]
  transfers between devices with their start and end apart: 10 -> 0, of which waited for: 7 -> 0; matrix products, arithmetic and copies ran while one was open for 8% -> 0% of each run, Pallas kernels for 0% -> 0%
where the time goes in v2:
time: 114 us
  Pallas kernels  110 us (96%)
  local copies, waits for them, and re-layouts  3.12 us (3%)
    pallas_call x1, Pallas kernels, layer(): pl.pallas_call(kernel, out_shape=(jax.ShapeDtypeStruct((OWN, WIDTH), bf16...  105 us
    pallas_call x1, Pallas kernels, finish(): pl.pallas_call(finish_kernel, out_shape=(jax.ShapeDtypeStruct(ordered.sha...  4.34 us
    unnamed x8, local copies, waits for them, and re-layouts  3.12 us

profile of v2, /device:TPU:1, one launch (start us, length us, event | category | flops | bytes accessed | tf_op | source)
XLA Modules:
  0.0 113.6 jit_solution(10532764354647159689)
XLA Ops:
  0.6 0.0 copy-start.2
  0.6 0.0 copy-start.3
  0.7 105.3 %layer.1 = (bf16[16,1792]{1,0:T(8,128)(2,1)}, bf16[8,448,576]{2,1,0:T(8,128)(2,1)}) custom-call(s32[256]{0:T(256)} %lengths.1, s32[2,2,32]{2,1,0:T(2,128)} %bitcast.7, bf16[16,1792]{1,0:T(8,128)(2,1)} %bitcast.12, f32[1792]{0:T(1024)} %refs_3_.1, bf16[576,1792]{1,0:T(8,128)(2,1)} %bitcast.9, bf16[2,8,32,576]{3,2,1,0:T(8,128)(2,1)} %refs_5_.1, ...), custom_call_target="tpu_custom_call" | custom-call | tf_op jit(solution)/shard_map/layer/pallas_call | solution.py:662
  106.0 0.0 copy-done.2
  106.0 0.0 copy-done.3
  106.0 0.0 copy-start
  106.0 2.3 %copy-done = bf16[8,448,576]{2,1,0:T(8,128)(2,1)S(1)} copy-done((bf16[8,448,576]{2,1,0:T(8,128)(2,1)S(1)}, bf16[8,448,576]{2,1,0:T(8,128)(2,1)}, u32[]{:S(2)}) %copy-start) | copy-done | bytes 4128792
  108.3 0.0 copy-start.1
  108.3 0.8 copy-done.1
  109.1 4.3 %finish.1 = (bf16[8,448,576]{2,1,0:T(8,128)(2,1)}, bf16[16,1792]{1,0:T(8,128)(2,1)}, s32[256]{0:T(256)}) custom-call(s32[256]{0:T(256)S(1)} %copy-done.3, s32[2,2,32]{2,1,0:T(2,128)S(1)} %bitcast.8, s32[1]{0:T(128)} %bitcast.1.group, bf16[8,448,576]{2,1,0:T(8,128)(2,1)S(1)} %copy-done, bf16[16,1792]{1,0:T(8,128)(2,1)S(1)} %copy-done.1), custom_call_target="tpu_custom_call" | custom-call | tf_op jit(solution)/shard_map/finish/pallas_call | solution.py:723
Async XLA Ops:
  0.6 105.3 %copy-start.2 = (s32[2,32,2]{1,2,0:T(2,128)S(1)}, s32[2,32,2]{1,2,0:T(2,128)}, u32[]{:S(2)}) copy-start(s32[2,32,2]{1,2,0:T(2,128)} %param.14) | copy-start | bytes 1540
  0.6 105.3 %copy-start.3 = (s32[256]{0:T(256)S(1)}, s32[256]{0:T(256)}, u32[]{:S(2)}) copy-start(s32[256]{0:T(256)} %lengths.1) | copy-start | bytes 3076
  106.0 2.3 %copy-start = (bf16[8,448,576]{2,1,0:T(8,128)(2,1)S(1)}, bf16[8,448,576]{2,1,0:T(8,128)(2,1)}, u32[]{:S(2)}) copy-start(bf16[8,448,576]{2,1,0:T(8,128)(2,1)} %get-tuple-element.8.ordered) | copy-start | bytes 12386308
  108.3 0.8 copy-start.1

commit v3 on v2

--- a/solution.py
+++ b/solution.py
@@ -27,8 +27,14 @@
 LAT = KVR + ROPE
 GROUPS = 2 * N * N
 EARLY = 4
+CAP = 448
+MOVE_PARTS = 4
+MOVE_ROWS = CAP // MOVE_PARTS
 NEAR_FIRST = (1, 3, 2)
 FAR_FIRST = (2, 1, 3)
+HOPS = (0, 1, 2, 1)
+CHIPS = sorted(range(1, N * N), key=lambda o: HOPS[o // N] + HOPS[o % N])
+SPARE = 64
 MESH = pl.DeviceIdType.MESH
 
 
@@ -48,31 +54,22 @@
         self.y = dp // (2 * N)
         self.z = (dp // 2) % N
         self.c = dp % 2
-        self.first = self.c * self.y + (1 - self.c) * self.z
-        self.second = self.c * self.z + (1 - self.c) * self.y
         self.me = dp
 
-    def group(self, y, z, c):
-        return y * (2 * N) + z * 2 + c
-
-    def on_first(self, k):
-        y = self.c * k + (1 - self.c) * self.y
-        z = self.c * self.z + (1 - self.c) * k
-        return {"dp": self.group(y, z, self.c), "tp": self.x}
-
-    def on_second(self, k):
-        y = self.c * self.y + (1 - self.c) * k
-        z = self.c * k + (1 - self.c) * self.z
-        return {"dp": self.group(y, z, self.c), "tp": self.x}
+    def on_chip(self, y, z):
+        return {"dp": y * (2 * N) + z * 2 + self.c, "tp": self.x}
 
     def on_core(self):
-        return {"dp": self.group(self.y, self.z, 1 - self.c), "tp": self.x}
+        return {"dp": self.me + 1 - 2 * self.c, "tp": self.x}
 
     def on_x(self, k):
         return {"dp": self.me, "tp": k}
 
     def on_ring(self, o):
         return {"dp": lax.rem(self.me + o + GROUPS, GROUPS), "tp": self.x}
+
+    def chip(self, offset):
+        return lax.rem(self.y + offset // N, N), lax.rem(self.z + offset % N, N)
 
 
 def remote(src, dst, send_sem, recv_sem, device):
@@ -114,6 +111,15 @@
             for first in (0, COLS)
         ]
         out[:, :, start : start + width] = jnp.concatenate(parts, axis=1).astype(jnp.bfloat16)
+
+
+def in_pieces(value):
+    pieces = []
+    for _ in range(3):
+        piece = value.astype(jnp.bfloat16).astype(jnp.float32)
+        pieces.append(piece)
+        value = value - piece
+    return pieces
 
 
 def source_of(moves, step, group, slot):
@@ -184,25 +190,31 @@
 def enter(here, barrier):
     devices = [here.on_ring(1), here.on_ring(-1), here.on_core()]
     for o in range(1, N):
-        devices.append(here.on_x(lax.rem(here.x + o, N)))
-        devices.append(here.on_first(lax.rem(here.first + o, N)))
-        devices.append(here.on_second(lax.rem(here.second + o, N)))
+        devices += [here.on_x(lax.rem(here.x + o, N)), here.on_chip(*here.chip(o)), here.on_chip(*here.chip(o * N))]
     for device in devices:
         pl.semaphore_signal(barrier, inc=1, device_id=device, device_id_type=MESH)
-
-    @pl.loop(0, GROUPS)
-    def _(i):
-        d = lax.rem(here.me + i, GROUPS)
-
-        @pl.when((d != here.me) | (here.x != here.y))
-        def _():
-            pl.semaphore_signal(barrier, inc=1, device_id={"dp": d, "tp": here.y}, device_id_type=MESH)
-
-    return len(devices) + GROUPS - 1 + jnp.where(here.x == here.y, 0, 1)
+    return len(devices)
+
+
+def tell(here, sem, line):
+    for device in known_line(here, line):
+        pl.semaphore_signal(sem, inc=1, device_id=device, device_id_type=MESH)
+
+
+def hear(here, sem, line):
+    pl.semaphore_wait(sem, len(known_line(here, line)))
+
+
+def known_line(here, line):
+    if line == "core":
+        return [here.on_core()]
+    if line == "x":
+        return [here.on_x(lax.rem(here.x + o, N)) for o in range(1, N)]
+    return [here.on_chip(*here.chip(o * N)) for o in range(1, N)]
 
 
 def head_copy(here, r, step, i):
-    place = here.c * BLOCKS + here.first * N + here.second
+    place = here.c * BLOCKS + here.y * N + here.z
     k = lax.rem(here.z * 2 + here.c + i // N, 2 * N)
     x = lax.rem(here.x + i, N)
     kept = (x == here.x) & (here.x * (2 * N) + k == here.me)
@@ -224,24 +236,24 @@
     return kept, copy, local
 
 
-def value_up(here, r, step, places):
-    for j in range(ROWS_DEV):
-        block = r.head_latent[step * ROWS_DEV + places[j]]
-        for c in range(KVR // 128):
-            r.head_sorted[c, j * HEADS : (j + 1) * HEADS, :] = block[:, c * 128 : (c + 1) * 128]
-
+def keep(r, line, row, result):
+    for c in range(KVR // 128):
+        r.head_latent[line, c, row * HEADS : (row + 1) * HEADS, :] = result[:, c * 128 : (c + 1) * 128]
+
+
+def value_up(here, r, line):
     def head(h):
         rows = jnp.concatenate(
-            [r.head_sorted.at[c][pl.ds(h, ROWS_DEV, stride=HEADS), :] for c in range(KVR // 128)], axis=1
+            [r.head_latent.at[line, c][pl.ds(h, ROWS_DEV, stride=HEADS), :] for c in range(KVR // 128)], axis=1
         ).astype(jnp.bfloat16)
         return jnp.dot(rows, r.vup[h], preferred_element_type=jnp.float32)
 
     for h in range(0, HEADS, 2):
-        r.heads[step, h // N, h % N // 2] = jnp.concatenate([head(h), head(h + 1)], axis=0).astype(jnp.bfloat16)
+        r.heads[line, h // N, h % N // 2] = jnp.concatenate([head(h), head(h + 1)], axis=0).astype(jnp.bfloat16)
 
     @pl.loop(0, GROUPS)
     def _(i):
-        kept, copy, local = head_copy(here, r, step, i)
+        kept, copy, local = head_copy(here, r, line, i)
 
         @pl.when(kept)
         def _():
@@ -253,44 +265,62 @@
 
 
 def front_line(here, r):
-    loads = []
-    for i, (src, dst) in enumerate(
+    loads = {}
+    for i, (name, src, dst) in enumerate(
         (
-            (r.cache_hbm, r.cache),
-            (r.lw_hbm, r.lw),
-            (r.queries_hbm, r.queries),
-            (r.vup_hbm, r.vup),
-            (r.wo_hbm, r.wo),
-            (r.wg_hbm, r.wg),
-            (r.wu_hbm, r.wu),
-            (r.wd_hbm, r.wd),
+            ("lw", r.lw_hbm, r.lw),
+            ("queries", r.queries_hbm, r.queries),
+            ("vup", r.vup_hbm, r.vup),
+            ("wo", r.wo_hbm, r.wo),
+            ("wg", r.wg_hbm, r.wg.at[pl.ds(0, FF_DEV)]),
+            ("wu", r.wu_hbm, r.wu),
+            ("wd", r.wd_hbm, r.wd),
         )
     ):
-        load = pltpu.make_async_copy(src, dst, r.load_sem.at[i])
+        loads[name] = pltpu.make_async_copy(src, dst, r.load_sem.at[i])
+    r.loads = loads
+    slot_loads = [
+        pltpu.make_async_copy(r.cache_hbm.at[j], r.cache.at[j], r.cache_sem.at[j]) for j in range(ROWS_DEV)
+    ]
+    for load in slot_loads:
         load.start()
-        loads.append(load)
-    r.weight_loads = loads[4:]
+    loads["lw"].start()
     barrier = pltpu.get_barrier_semaphore()
     entered = enter(here, barrier)
 
     moves, me = r.moves, here.me
     a0, b0, a1, b1 = moves[0, 0, me], moves[0, 1, me], moves[1, 0, me], moves[1, 1, me]
     slots, places = slot_order(moves, me)
-
-    loads[0].wait()
+    r.slots, r.places = slots, places
+    r.wg[pl.ds(FF_DEV, SPARE), :] = jnp.zeros((SPARE, WIDTH), jnp.bfloat16)
+    wide = r.tokens[...].astype(jnp.float32)
+    r.tokens_wide[...] = wide
+    r.latents[...] = jnp.zeros_like(r.latents)
+    r.latents[:, LAT + 64 :] = jnp.broadcast_to(jnp.sum(wide * wide, axis=1, keepdims=True), (OWN, 128))
+
+    def move(leaving, arrived, sem, part):
+        rows = pl.ds(part * MOVE_ROWS, MOVE_ROWS)
+        return [
+            send(
+                leaving.at[i, rows],
+                arrived.at[i, rows],
+                sem.at[0, i, part],
+                sem.at[1, i, part],
+                here.on_ring(o),
+            )
+            for i, o in enumerate((1, -1))
+        ]
+
+    for load in slot_loads:
+        load.wait()
     r.leaving0[0] = r.cache[a0]
     r.leaving0[1] = r.cache[b0]
     pl.semaphore_wait(barrier, entered)
-    moving0 = [
-        send(r.leaving0.at[i], r.arrived0.at[i], r.move0_sem.at[0, i], r.move0_sem.at[1, i], here.on_ring(o))
-        for i, o in enumerate((1, -1))
-    ]
-
-    loads[1].wait()
-    wide = r.tokens[...].astype(jnp.float32)
-    r.latents[...] = jnp.zeros_like(r.latents)
+    tell(here, r.y_in, "y")
+    moving0 = [move(r.leaving0, r.arrived0, r.move0_sem, part) for part in range(MOVE_PARTS)]
+
+    loads["lw"].wait()
     r.latents[:, :LAT] = dot_rows(r.tokens[...], r.lw[...])
-    r.latents[:, LAT + 64 :] = jnp.broadcast_to(jnp.sum(wide * wide, axis=1, keepdims=True), (OWN, 128))
     copies = [
         send(
             r.latents,
@@ -301,6 +331,8 @@
         )
         for o in FAR_FIRST
     ]
+    for name in ("queries", "vup", "wo", "wg", "wu", "wd"):
+        loads[name].start()
     held = [held_first(r.lengths, moves, me, j) for j in range(ROWS_DEV)]
     held += [held_second(r.lengths, moves, me, j) for j in range(ROWS_DEV)]
     row = lax.broadcasted_iota(jnp.int32, (OWN, 128), 0)
@@ -314,7 +346,10 @@
             result = jnp.where(slots[place] == j, held[step * ROWS_DEV + j], result)
         return result
 
-    yield
+    held_by_place = [[held_at(step, p) for p in range(ROWS_DEV)] for step in range(STEPS)]
+    yield
+    hear(here, r.y_in, "y")
+    tell(here, r.x_in, "x")
     for copy in copies:
         copy.wait()
     total = r.latents[...]
@@ -328,102 +363,108 @@
     def fresh_row(step, place):
         return r.fresh[pl.ds(step * ROWS_DEV + slots[place], 1), :LAT].astype(jnp.bfloat16)
 
-    loads[2].wait()
+    loads["queries"].wait()
     r.ordered_copies = []
+
+    def put_out(ref, place):
+        copy = pltpu.make_async_copy(ref, r.ordered.at[place], r.out_sem.at[place])
+        copy.start()
+        r.ordered_copies.append(copy)
+
     for p in range(EARLY):
-        first, second = held_at(0, p), held_at(1, p)
+        first, second = held_by_place[0][p], held_by_place[1][p]
         block = with_row(r.cache[slots[p]], first, fresh_row(0, p))
         r.early_keys[p] = with_row(block, second, fresh_row(1, p))
-        copy = pltpu.make_async_copy(r.early_keys.at[p], r.ordered.at[p], r.out_sem.at[p])
-        copy.start()
-        r.ordered_copies.append(copy)
+        put_out(r.early_keys.at[p], p)
         rows = jnp.concatenate([r.queries[0, slots[p]], r.queries[1, slots[p]]], axis=0)
         step_row = lax.broadcasted_iota(jnp.int32, (2 * HEADS, 1), 0)
         live = jnp.where(step_row < HEADS, first + 1, second + 1)
         result = attend(rows, r.early_keys.at[p], live)
-        r.head_latent[p] = result[:HEADS]
-        r.head_latent[ROWS_DEV + p] = result[HEADS:]
-
-    yield
-    for copy in moving0:
-        copy.wait()
-    for p in range(EARLY, ROWS_DEV):
-        block = jnp.where(
-            slots[p] == a0, r.arrived0[1], jnp.where(slots[p] == b0, r.arrived0[0], r.cache[slots[p]])
-        )
-        r.keys0[p - EARLY] = with_row(block, held_at(0, p), fresh_row(0, p))
+        keep(r, 0, p, result[:HEADS])
+        keep(r, 0, EARLY + p, result[HEADS:])
+
+    yield
+    hear(here, r.x_in, "x")
+    tell(here, r.core_in, "core")
     place_a, place_b = 0, 0
     for p in range(EARLY, ROWS_DEV):
         place_a = jnp.where(slots[p] == a1, p - EARLY, place_a)
         place_b = jnp.where(slots[p] == b1, p - EARLY, place_b)
-    r.leaving1[0] = r.keys0[place_a]
-    r.leaving1[1] = r.keys0[place_b]
-    moving1 = [
-        send(r.leaving1.at[i], r.arrived1.at[i], r.move1_sem.at[0, i], r.move1_sem.at[1, i], here.on_ring(o))
-        for i, o in enumerate((1, -1))
-    ]
+
+    def arrive(step, keys, part, arrived, own_a, own_b, kept):
+        rows = pl.ds(part * MOVE_ROWS, MOVE_ROWS)
+        for p in range(EARLY, ROWS_DEV):
+            block = jnp.where(
+                slots[p] == own_a,
+                arrived[1, rows],
+                jnp.where(slots[p] == own_b, arrived[0, rows], kept(p, rows)),
+            )
+            keys[p - EARLY, rows] = with_row(
+                block, held_by_place[step][p] - part * MOVE_ROWS, fresh_row(step, p)
+            )
+
+    moving1 = []
+    for part in range(MOVE_PARTS):
+        rows = pl.ds(part * MOVE_ROWS, MOVE_ROWS)
+        for copy in moving0[part]:
+            copy.wait()
+        arrive(0, r.keys0, part, r.arrived0, a0, b0, lambda p, rows: r.cache[slots[p], rows])
+        r.leaving1[0, rows] = r.keys0[place_a, rows]
+        r.leaving1[1, rows] = r.keys0[place_b, rows]
+        moving1.append(move(r.leaving1, r.arrived1, r.move1_sem, part))
+    yield
+    loads["vup"].wait()
+    hear(here, r.core_in, "core")
+    value_up(here, r, 0)
+    yield
     for p in range(EARLY, ROWS_DEV):
-        r.head_latent[p] = attend(r.queries[0, slots[p]], r.keys0.at[p - EARLY], held_at(0, p) + 1)
-    loads[3].wait()
-    value_up(here, r, 0, places)
-
-    yield
-    for copy in moving1:
-        copy.wait()
+        keep(
+            r, 1, p - EARLY,
+            attend(r.queries[0, slots[p]], r.keys0.at[p - EARLY], held_by_place[0][p] + 1),
+        )
+
+    yield
+    for part in range(MOVE_PARTS):
+        for copy in moving1[part]:
+            copy.wait()
+        arrive(1, r.keys1, part, r.arrived1, a1, b1, lambda p, rows: r.keys0[p - EARLY, rows])
     for p in range(EARLY, ROWS_DEV):
-        block = jnp.where(
-            slots[p] == a1, r.arrived1[1], jnp.where(slots[p] == b1, r.arrived1[0], r.keys0[p - EARLY])
+        put_out(r.keys1.at[p - EARLY], p)
+        keep(
+            r, 1, p,
+            attend(r.queries[1, slots[p]], r.keys1.at[p - EARLY], held_by_place[1][p] + 1),
         )
-        r.keys1[p - EARLY] = with_row(block, held_at(1, p), fresh_row(1, p))
-        copy = pltpu.make_async_copy(r.keys1.at[p - EARLY], r.ordered.at[p], r.out_sem.at[p])
-        copy.start()
-        r.ordered_copies.append(copy)
-    for p in range(EARLY, ROWS_DEV):
-        r.head_latent[ROWS_DEV + p] = attend(
-            r.queries[1, slots[p]], r.keys1.at[p - EARLY], held_at(1, p) + 1
-        )
-    yield
-    value_up(here, r, 1, places)
+    yield
+    value_up(here, r, 1)
     yield
 
 
 def reduce_over_groups(here, r, step, use):
     own, peer = r.own.at[step], r.peer_rows.at[use, step]
-    core_sem, sem1, sem2 = r.core_sem.at[use, step], r.sem1.at[use, step], r.sem2.at[use, step]
-    sums, parts, rows1, rows2 = r.sums.at[step], r.parts.at[step], r.rows1.at[use, step], r.rows2.at[use, step]
-    remote(r.to_peer.at[step], peer, core_sem.at[0], core_sem.at[1], here.on_core()).wait()
-
-    def both(k):
-        blocks = pl.ds(k * N, N)
-        return own[blocks].astype(jnp.float32) + peer[blocks].astype(jnp.float32)
-
+    sem = r.sum_sem.at[use, step]
+    sums, rows = r.sums.at[step], r.rows.at[use, step]
+    r.core_copy[use, step].wait()
     copies = {}
-    for o in FAR_FIRST:
-        k = lax.rem(here.first + o, N)
-        sums[k] = both(k).astype(jnp.bfloat16)
-        copies[o] = send(sums.at[k], rows1.at[o - 1], sem1.at[0, o - 1], sem1.at[1, o - 1], here.on_first(k))
-    total = both(here.first)
-    yield
-    for o in NEAR_FIRST:
+    for o in reversed(CHIPS):
+        y, z = here.chip(o)
+        k = y * N + z
+        sums[k] = (own[k].astype(jnp.float32) + peer[k].astype(jnp.float32)).astype(jnp.bfloat16)
+        copies[o] = send(sums.at[k], rows.at[o], sem.at[0, o], sem.at[1, o], here.on_chip(y, z))
+    k = here.y * N + here.z
+    total = own[k].astype(jnp.float32) + peer[k].astype(jnp.float32)
+    yield
+    for o in CHIPS:
         copies[o].wait()
-        total = total + rows1[o - 1].astype(jnp.float32)
-    parts[...] = total.astype(jnp.bfloat16)
-    copies = {}
-    for o in FAR_FIRST:
-        k = lax.rem(here.second + o, N)
-        copies[o] = send(parts.at[k], rows2.at[o - 1], sem2.at[0, o - 1], sem2.at[1, o - 1], here.on_second(k))
-    yield
-    total = parts[here.second].astype(jnp.float32)
-    for o in NEAR_FIRST:
-        copies[o].wait()
-        total = total + rows2[o - 1].astype(jnp.float32)
+        total = total + rows[o].astype(jnp.float32)
     return total
 
 
 def project_both(here, r, step, use, lhs, weight):
     project(lhs(1 - here.c), weight, r.to_peer.at[step])
     core_sem = r.core_sem.at[use, step]
-    send(r.to_peer.at[step], r.peer_rows.at[use, step], core_sem.at[0], core_sem.at[1], here.on_core())
+    r.core_copy[use, step] = send(
+        r.to_peer.at[step], r.peer_rows.at[use, step], core_sem.at[0], core_sem.at[1], here.on_core()
+    )
     project(lhs(here.c), weight, r.own.at[step])
 
 
@@ -449,7 +490,7 @@
             rows[:, h // 2, first : first + ROWS_DEV].reshape(2 * HALF, HD).astype(bf16)
         )
     if step == 0:
-        r.weight_loads[0].wait()
+        r.loads["wo"].wait()
 
     def half(ref, c):
         return ref[pl.ds(pl.multiple_of(c * HALF, HALF), HALF), :]
@@ -457,54 +498,32 @@
     project_both(here, r, step, 0, lambda c: half(r.head_block, c), r.wo[...])
     yield
     attention = yield from reduce_over_groups(here, r, step, 0)
-    tokens = stacked(r.tokens[...].astype(f32)[step * ROWS_DEV : (step + 1) * ROWS_DEV])[0]
+    for i in range(ROWS_DEV):
+        token = i // EARLY * ROWS_DEV + r.slots[step * EARLY + i % EARLY]
+        r.line_tokens[step, i : i + 1, :] = r.tokens_wide[pl.ds(token, 1), :]
+    tokens = stacked(r.line_tokens[step])[0]
     mixed = (tokens + attention).astype(bf16).astype(f32)
     r.mixed[step] = mixed
 
-    squares = jnp.sum(mixed * mixed, axis=1, keepdims=True)
-    squares = squares[:ROWS_DEV] + squares[ROWS_DEV:]
-    norms, norm_rows, sem = r.norms.at[step], r.norm_rows.at[step], r.norm_sem.at[step]
-    norms[...] = jnp.broadcast_to(squares, norms.shape)
+    mixed_all = r.mixed_all.at[step]
+    mine = mixed_all.at[here.c, here.y, here.z]
+    mine[...] = mixed.astype(bf16)
+    sem, core_sem = r.gather_sem.at[step], r.gather_core.at[step]
     copies = {}
-    for o in FAR_FIRST:
-        x = lax.rem(here.x + o, N)
-        copies[o] = send(norms, norm_rows.at[o - 1], sem.at[0, o - 1], sem.at[1, o - 1], here.on_x(x))
-    yield
-    squares = norms[...]
-    for o in NEAR_FIRST:
-        copies[o].wait()
-        squares = squares + norm_rows[o - 1]
-    scale = lax.rsqrt(squares / D + epsilon)[:, :1]
-    scale = jnp.concatenate([scale, scale], axis=0)
-    gain = stacked(jnp.broadcast_to(r.gain[...].reshape(1, WIDTH), (ROWS_DEV, WIDTH)))[0]
-    mixed_all = r.mixed_all.at[step]
-    mixed_all[here.c, here.first, here.second] = (r.mixed[step] * gain * scale).astype(bf16)
-
-    mine = mixed_all.at[here.c, here.first, here.second]
-    sem = r.gather2.at[step]
-    copies = {}
-    for o in FAR_FIRST:
-        k = lax.rem(here.second + o, N)
-        copies[o] = send(mine, mine, sem.at[0, o - 1], sem.at[1, o - 1], here.on_second(k))
-    yield
-    for o in NEAR_FIRST:
-        copies[o].wait()
-    mine = mixed_all.at[here.c, here.first]
-    sem, core_sem = r.gather1.at[step], r.gather_core.at[step]
-    copies = {}
-    for o in FAR_FIRST:
-        k = lax.rem(here.first + o, N)
-        copies[o] = send(mine, mine, sem.at[0, o - 1], sem.at[1, o - 1], here.on_first(k))
-    handed = [send(mine, mine, core_sem.at[0, 0], core_sem.at[1, 0], here.on_core())]
-    yield
-    for o in NEAR_FIRST:
-        copies[o].wait()
-        block = mixed_all.at[here.c, lax.rem(here.first + N - o, N)]
+    for o in reversed(CHIPS):
+        copies[o] = send(mine, mine, sem.at[0, o], sem.at[1, o], here.on_chip(*here.chip(o)))
+    yield
+    handed = []
+    for o in (0, *NEAR_FIRST):
+        for i in range(N):
+            if o + i:
+                copies[o * N + i].wait()
+        block = mixed_all.at[here.c, lax.rem(here.y + N - o, N)]
         handed.append(send(block, block, core_sem.at[0, o], core_sem.at[1, o], here.on_core()))
 
     if step == 0:
-        r.weight_loads[1].wait()
-        r.weight_loads[2].wait()
+        r.loads["wg"].wait()
+        r.loads["wu"].wait()
     sums = (
         (r.gate_part.at[step], r.gate_rows.at[step], r.gate_sem.at[step], r.wg),
         (r.up_part.at[step], r.up_rows.at[step], r.up_sem.at[step], r.wu),
@@ -519,9 +538,16 @@
             yield
             for copy in handed:
                 copy.wait()
-        r.lhs[...] = unstacked(mixed_all[core].astype(f32).reshape(BLOCKS, TILE, COLS)).astype(bf16)
+        wide = unstacked(mixed_all[core].astype(f32).reshape(BLOCKS, TILE, COLS))
+        r.lhs[...] = (wide * r.gain[...].reshape(1, WIDTH)).astype(bf16)
+        pieces = in_pieces(jnp.sum(wide * wide, axis=1, keepdims=True))
         for part, rows, sem, weight in sums:
-            part[pl.ds(2 * core, 2)] = dot_rows(r.lhs[...], weight[...]).astype(bf16).reshape(2, CHUNK, FF_DEV)
+            result = dot_rows(r.lhs[...], weight[...])
+            if weight is r.wg:
+                lane = lax.broadcasted_iota(jnp.int32, result.shape, 1)
+                for i, piece in enumerate(pieces):
+                    result = jnp.where(lane == FF_DEV + i, piece, result)
+            part[pl.ds(2 * core, 2)] = result.astype(bf16).reshape(2, CHUNK, -1)
             for i in range(2):
                 k = 2 * core + lax.rem(here.x + i, 2)
 
@@ -539,6 +565,10 @@
             total = total + rows[o].astype(f32)
         totals.append(total)
     gate, up = totals
+    lane = lax.broadcasted_iota(jnp.int32, gate.shape, 1)
+    squares = jnp.sum(jnp.where(lane >= FF_DEV, gate, 0.0), axis=1, keepdims=True)
+    scale = lax.rsqrt(squares / D + epsilon)
+    gate, up = gate[:, :FF_DEV] * scale, up * scale
     activation = r.activation.at[step]
     activation[here.x] = (gate / (1.0 + jnp.exp(-gate)) * up).astype(bf16)
     mine = activation.at[here.x]
@@ -552,17 +582,17 @@
         copies[o].wait()
 
     if step == 0:
-        r.weight_loads[3].wait()
+        r.loads["wd"].wait()
     project_both(
         here, r, step, 1, lambda c: activation[pl.ds(2 * c, 2)].reshape(HALF, FF_DEV), r.wd[...]
     )
     yield
     down = yield from reduce_over_groups(here, r, step, 1)
-    r.results[step] = unstacked((r.mixed[step] + down)[None])
-    yield
-
-
-ORDER = "FFFF0F001010101010101010101010111"
+    r.results[step * ROWS_DEV : (step + 1) * ROWS_DEV, :] = unstacked((r.mixed[step] + down)[None])
+    yield
+
+
+ORDER = "FFFFF00FF0110010110010111"
 
 INPUTS = (
     "lengths", "moves", "tokens", "gain", "lw_hbm", "queries_hbm", "cache_hbm", "vup_hbm",
@@ -572,11 +602,16 @@
 
 def layer_kernel(names, *refs):
     r = types.SimpleNamespace(**dict(zip(names, refs)))
+    r.core_copy = {}
     here = Place()
     lines = {"F": front_line(here, r), "0": back_line(here, r, 0), "1": back_line(here, r, 1)}
     for name in ORDER:
         next(lines[name], None)
-    r.out[...] = jnp.concatenate([r.results[0], r.results[1]], axis=0).astype(jnp.bfloat16)
+    for i in range(OWN):
+        place = r.places[i % ROWS_DEV]
+        row = place // EARLY * ROWS_DEV + i // ROWS_DEV * EARLY + lax.rem(place, EARLY)
+        r.sorted_results[i : i + 1, :] = r.results[pl.ds(row, 1), :]
+    r.out[...] = r.sorted_results[...].astype(jnp.bfloat16)
     for copy in r.ordered_copies:
         copy.wait()
 
@@ -600,7 +635,7 @@
         queries=held(*queries.shape),
         vup=held(*vup.shape),
         wo=held(*wo.shape),
-        wg=held(*wg.shape),
+        wg=held(FF_DEV + SPARE, WIDTH),
         wu=held(*wu.shape),
         wd=held(*wd.shape),
         latents=held(OWN, LAT + 64 + 128, dtype=f32),
@@ -613,42 +648,41 @@
         early_keys=held(EARLY, *slot),
         keys0=held(ROWS_DEV - EARLY, *slot),
         keys1=held(ROWS_DEV - EARLY, *slot),
-        head_latent=held(OWN, HEADS, KVR, dtype=f32),
-        head_sorted=held(KVR // 128, ROWS_DEV * HEADS, 128, dtype=f32),
+        head_latent=held(2, KVR // 128, ROWS_DEV * HEADS, 128, dtype=f32),
         heads=held(STEPS, 2 * N, N // 2, TILE, HD),
         head_rows=held(STEPS, GROUPS, N // 2, TILE, HD),
         head_block=held(2 * HALF, N * HD),
         to_peer=held(STEPS, BLOCKS, TILE, COLS),
         own=held(STEPS, BLOCKS, TILE, COLS),
         peer_rows=held(2, STEPS, BLOCKS, TILE, COLS),
-        sums=held(STEPS, N, N, TILE, COLS),
-        parts=held(STEPS, N, TILE, COLS),
-        rows1=held(2, STEPS, N - 1, N, TILE, COLS),
-        rows2=held(2, STEPS, N - 1, TILE, COLS),
+        sums=held(STEPS, BLOCKS, TILE, COLS),
+        rows=held(2, STEPS, BLOCKS, TILE, COLS),
         mixed=held(STEPS, TILE, COLS, dtype=f32),
-        norms=held(STEPS, ROWS_DEV, 128, dtype=f32),
-        norm_rows=held(STEPS, N - 1, ROWS_DEV, 128, dtype=f32),
         mixed_all=held(STEPS, 2, N, N, TILE, COLS),
         lhs=held(HALF, WIDTH),
-        gate_part=held(STEPS, N, CHUNK, FF_DEV),
+        gate_part=held(STEPS, N, CHUNK, FF_DEV + SPARE),
         up_part=held(STEPS, N, CHUNK, FF_DEV),
-        gate_rows=held(STEPS, N - 1, CHUNK, FF_DEV),
+        gate_rows=held(STEPS, N - 1, CHUNK, FF_DEV + SPARE),
         up_rows=held(STEPS, N - 1, CHUNK, FF_DEV),
         activation=held(STEPS, N, CHUNK, FF_DEV),
-        results=held(STEPS, ROWS_DEV, WIDTH, dtype=f32),
-        load_sem=dma(8),
+        results=held(OWN, WIDTH, dtype=f32),
+        sorted_results=held(OWN, WIDTH, dtype=f32),
+        tokens_wide=held(OWN, WIDTH, dtype=f32),
+        line_tokens=held(2, ROWS_DEV, WIDTH, dtype=f32),
+        y_in=pltpu.SemaphoreType.REGULAR,
+        x_in=pltpu.SemaphoreType.REGULAR,
+        core_in=pltpu.SemaphoreType.REGULAR,
+        load_sem=dma(7),
+        cache_sem=dma(ROWS_DEV),
         latent_sem=dma(2, N - 1),
-        move0_sem=dma(2, 2),
-        move1_sem=dma(2, 2),
+        move0_sem=dma(2, 2, MOVE_PARTS),
+        move1_sem=dma(2, 2, MOVE_PARTS),
         out_sem=dma(ROWS_DEV),
         head_send=dma(STEPS, GROUPS),
         head_recv=dma(STEPS, GROUPS),
         core_sem=dma(2, STEPS, 2),
-        sem1=dma(2, STEPS, 2, N - 1),
-        sem2=dma(2, STEPS, 2, N - 1),
-        norm_sem=dma(STEPS, 2, N - 1),
-        gather2=dma(STEPS, 2, N - 1),
-        gather1=dma(STEPS, 2, N - 1),
+        sum_sem=dma(2, STEPS, 2, BLOCKS),
+        gather_sem=dma(STEPS, 2, BLOCKS),
         gather_core=dma(STEPS, 2, N),
         gate_sem=dma(STEPS, 2, N - 1),
         up_sem=dma(STEPS, 2, N - 1),
@@ -685,14 +719,18 @@
     stores.append(pltpu.make_async_copy(row_block, final_rows, row_sem.at[1]))
     for load in loads:
         load.start()
-    for load, store in zip(loads, stores):
-        load.wait()
-        store.start()
+
+    def pass_on(first, last):
+        for load, store in zip(loads[first:last], stores[first:last]):
+            load.wait()
+            store.start()
 
     @pl.loop(0, GROUPS)
     def _(g):
         for j in range(ROWS_DEV):
             moved[g * ROWS_DEV + j] = lengths[g * ROWS_DEV + j] + 1
+
+    pass_on(0, 3)
 
     @pl.loop(0, GROUPS)
     def _(g):
@@ -700,6 +738,8 @@
         left = lax.rem(g + GROUPS - 1, GROUPS)
         moved[g * ROWS_DEV + moves[0, 0, g]] = lengths[right * ROWS_DEV + moves[0, 1, right]] + 1
         moved[g * ROWS_DEV + moves[0, 1, g]] = lengths[left * ROWS_DEV + moves[0, 0, left]] + 1
+
+    pass_on(3, ROWS_DEV + 1)
 
     @pl.loop(0, GROUPS)
     def _(g):
@@ -736,7 +776,7 @@
             pltpu.SemaphoreType.DMA((2, ROWS_DEV)),
             pltpu.SemaphoreType.DMA((2,)),
         ],
-        compiler_params=pltpu.CompilerParams(vmem_limit_bytes=16 * 1024 * 1024),
+        compiler_params=pltpu.CompilerParams(vmem_limit_bytes=60 * 1024 * 1024),
         name="finish",
     )(lengths, moves, group, ordered, rows)
 

time: 114 us -> 101 us (0.89)
  Pallas kernels: 110 us -> 100 us
  local copies, waits for them, and re-layouts: 3.12 us -> 0 us
    pallas_call x1, Pallas kernels: 105 us -> 94.8 us  [layer(): pl.pallas_call(kernel, out_shape=(jax.ShapeDtypeStruct((OWN, WIDTH), bf16...]
    unnamed x8 -> x0, local copies, waits for them, and re-layouts: 3.12 us -> none
where the time goes in v3:
time: 101 us
  Pallas kernels  100 us (99%)
    pallas_call x1, Pallas kernels, layer(): pl.pallas_call(kernel, out_shape=(jax.ShapeDtypeStruct((OWN, WIDTH), bf16...  94.8 us
    pallas_call x1, Pallas kernels, finish(): pl.pallas_call(finish_kernel, out_shape=(jax.ShapeDtypeStruct(ordered.sha...  5.35 us

profile of v3, /device:TPU:1, one launch (start us, length us, event | category | flops | bytes accessed | tf_op | source)
XLA Modules:
  0.0 101.0 jit_solution(2885559869063060455)
XLA Ops:
  0.6 94.8 %layer.1 = (bf16[16,1792]{1,0:T(8,128)(2,1)}, bf16[8,448,576]{2,1,0:T(8,128)(2,1)}) custom-call(s32[256]{0:T(256)} %lengths.1, s32[2,2,32]{2,1,0:T(2,128)} %bitcast.11, bf16[16,1792]{1,0:T(8,128)(2,1)} %bitcast.10, f32[1792]{0:T(1024)} %refs_3_.1, bf16[576,1792]{1,0:T(8,128)(2,1)} %bitcast.7, bf16[2,8,32,576]{3,2,1,0:T(8,128)(2,1)} %refs_5_.1, ...), custom_call_target="tpu_custom_call" | custom-call | tf_op jit(solution)/shard_map/layer/pallas_call | solution.py:696
  95.5 5.4 %finish.1 = (bf16[8,448,576]{2,1,0:T(8,128)(2,1)}, bf16[16,1792]{1,0:T(8,128)(2,1)}, s32[256]{0:T(256)}) custom-call(s32[256]{0:T(256)} %lengths.1, s32[2,2,32]{2,1,0:T(2,128)} %bitcast.12, s32[1]{0:T(128)} %bitcast.1.group, bf16[8,448,576]{2,1,0:T(8,128)(2,1)} %get-tuple-element.8.ordered, bf16[16,1792]{1,0:T(8,128)(2,1)} %get-tuple-element.9.rows), custom_call_target="tpu_custom_call" | custom-call | tf_op jit(solution)/shard_map/finish/pallas_call | solution.py:763

commit v4 on v3

--- a/solution.py
+++ b/solution.py
@@ -364,22 +364,14 @@
         return r.fresh[pl.ds(step * ROWS_DEV + slots[place], 1), :LAT].astype(jnp.bfloat16)
 
     loads["queries"].wait()
-    r.ordered_copies = []
-
-    def put_out(ref, place):
-        copy = pltpu.make_async_copy(ref, r.ordered.at[place], r.out_sem.at[place])
-        copy.start()
-        r.ordered_copies.append(copy)
-
     for p in range(EARLY):
         first, second = held_by_place[0][p], held_by_place[1][p]
         block = with_row(r.cache[slots[p]], first, fresh_row(0, p))
-        r.early_keys[p] = with_row(block, second, fresh_row(1, p))
-        put_out(r.early_keys.at[p], p)
+        r.ordered[p][...] = with_row(block, second, fresh_row(1, p))
         rows = jnp.concatenate([r.queries[0, slots[p]], r.queries[1, slots[p]]], axis=0)
         step_row = lax.broadcasted_iota(jnp.int32, (2 * HEADS, 1), 0)
         live = jnp.where(step_row < HEADS, first + 1, second + 1)
-        result = attend(rows, r.early_keys.at[p], live)
+        result = attend(rows, r.ordered[p], live)
         keep(r, 0, p, result[:HEADS])
         keep(r, 0, EARLY + p, result[HEADS:])
 
@@ -399,7 +391,7 @@
                 arrived[1, rows],
                 jnp.where(slots[p] == own_b, arrived[0, rows], kept(p, rows)),
             )
-            keys[p - EARLY, rows] = with_row(
+            keys[p][rows] = with_row(
                 block, held_by_place[step][p] - part * MOVE_ROWS, fresh_row(step, p)
             )
 
@@ -408,7 +400,7 @@
         rows = pl.ds(part * MOVE_ROWS, MOVE_ROWS)
         for copy in moving0[part]:
             copy.wait()
-        arrive(0, r.keys0, part, r.arrived0, a0, b0, lambda p, rows: r.cache[slots[p], rows])
+        arrive(0, {p: r.keys0.at[p - EARLY] for p in range(EARLY, ROWS_DEV)}, part, r.arrived0, a0, b0, lambda p, rows: r.cache[slots[p], rows])
         r.leaving1[0, rows] = r.keys0[place_a, rows]
         r.leaving1[1, rows] = r.keys0[place_b, rows]
         moving1.append(move(r.leaving1, r.arrived1, r.move1_sem, part))
@@ -427,12 +419,11 @@
     for part in range(MOVE_PARTS):
         for copy in moving1[part]:
             copy.wait()
-        arrive(1, r.keys1, part, r.arrived1, a1, b1, lambda p, rows: r.keys0[p - EARLY, rows])
+        arrive(1, r.ordered, part, r.arrived1, a1, b1, lambda p, rows: r.keys0[p - EARLY, rows])
     for p in range(EARLY, ROWS_DEV):
-        put_out(r.keys1.at[p - EARLY], p)
         keep(
             r, 1, p,
-            attend(r.queries[1, slots[p]], r.keys1.at[p - EARLY], held_by_place[1][p] + 1),
+            attend(r.queries[1, slots[p]], r.ordered[p], held_by_place[1][p] + 1),
         )
     yield
     value_up(here, r, 1)
@@ -603,6 +594,7 @@
 def layer_kernel(names, *refs):
     r = types.SimpleNamespace(**dict(zip(names, refs)))
     r.core_copy = {}
+    r.ordered = [getattr(r, f"ordered{p}") for p in range(ROWS_DEV)]
     here = Place()
     lines = {"F": front_line(here, r), "0": back_line(here, r, 0), "1": back_line(here, r, 1)}
     for name in ORDER:
@@ -612,8 +604,6 @@
         row = place // EARLY * ROWS_DEV + i // ROWS_DEV * EARLY + lax.rem(place, EARLY)
         r.sorted_results[i : i + 1, :] = r.results[pl.ds(row, 1), :]
     r.out[...] = r.sorted_results[...].astype(jnp.bfloat16)
-    for copy in r.ordered_copies:
-        copy.wait()
 
 
 def layer(lengths, moves, tokens, gain, lw, queries, cache, vup, wo, wg, wu, wd):
@@ -645,9 +635,7 @@
         leaving1=held(2, *slot),
         arrived0=held(2, *slot),
         arrived1=held(2, *slot),
-        early_keys=held(EARLY, *slot),
         keys0=held(ROWS_DEV - EARLY, *slot),
-        keys1=held(ROWS_DEV - EARLY, *slot),
         head_latent=held(2, KVR // 128, ROWS_DEV * HEADS, 128, dtype=f32),
         heads=held(STEPS, 2 * N, N // 2, TILE, HD),
         head_rows=held(STEPS, GROUPS, N // 2, TILE, HD),
@@ -677,7 +665,6 @@
         latent_sem=dma(2, N - 1),
         move0_sem=dma(2, 2, MOVE_PARTS),
         move1_sem=dma(2, 2, MOVE_PARTS),
-        out_sem=dma(ROWS_DEV),
         head_send=dma(STEPS, GROUPS),
         head_recv=dma(STEPS, GROUPS),
         core_sem=dma(2, STEPS, 2),
@@ -688,7 +675,7 @@
         up_sem=dma(STEPS, 2, N - 1),
         act_sem=dma(STEPS, 2, N - 1),
     )
-    names = (*INPUTS, "out", "ordered", *scratch)
+    names = (*INPUTS, "out", *(f"ordered{p}" for p in range(ROWS_DEV)), *scratch)
 
     def kernel(*refs):
         layer_kernel(names, *refs)
@@ -697,40 +684,33 @@
         kernel,
         out_shape=(
             jax.ShapeDtypeStruct((OWN, WIDTH), bf16),
-            jax.ShapeDtypeStruct(cache.shape, bf16),
+            *[jax.ShapeDtypeStruct(slot, bf16)] * ROWS_DEV,
         ),
         in_specs=[smem, smem, vmem, vmem] + [hbm] * 8,
-        out_specs=(vmem, hbm),
+        out_specs=(vmem, *[vmem] * ROWS_DEV),
         scratch_shapes=list(scratch.values()),
         compiler_params=pltpu.CompilerParams(
-            collective_id=0, has_side_effects=True, vmem_limit_bytes=58 * 1024 * 1024
+            collective_id=0, has_side_effects=True, vmem_limit_bytes=49 * 1024 * 1024
         ),
         name="layer",
     )(lengths, moves, tokens, gain, lw, queries, cache, vup, wo, wg, wu, wd)
 
 
-def finish_kernel(
-    lengths, moves, group, ordered, rows, final_cache, final_rows, final_lengths, moved, slots, row_block, sems, row_sem
-):
-    _, places = slot_order(moves, group[0])
-    loads = [pltpu.make_async_copy(ordered.at[places[j]], slots.at[j], sems.at[0, j]) for j in range(ROWS_DEV)]
-    stores = [pltpu.make_async_copy(slots.at[j], final_cache.at[j], sems.at[1, j]) for j in range(ROWS_DEV)]
-    loads.append(pltpu.make_async_copy(rows, row_block, row_sem.at[0]))
-    stores.append(pltpu.make_async_copy(row_block, final_rows, row_sem.at[1]))
-    for load in loads:
-        load.start()
-
-    def pass_on(first, last):
-        for load, store in zip(loads[first:last], stores[first:last]):
-            load.wait()
-            store.start()
+def finish_kernel(lengths, moves, group, rows, *refs):
+    ordered, (final_cache, final_rows, final_lengths, moved, sems) = refs[:ROWS_DEV], refs[ROWS_DEV:]
+    slots, _ = slot_order(moves, group[0])
+    stores = [
+        pltpu.make_async_copy(ordered[p], final_cache.at[slots[p]], sems.at[p]) for p in range(ROWS_DEV)
+    ]
+    stores.append(pltpu.make_async_copy(rows, final_rows, sems.at[ROWS_DEV]))
+    for store in stores:
+        store.start()
 
     @pl.loop(0, GROUPS)
     def _(g):
         for j in range(ROWS_DEV):
             moved[g * ROWS_DEV + j] = lengths[g * ROWS_DEV + j] + 1
 
-    pass_on(0, 3)
 
     @pl.loop(0, GROUPS)
     def _(g):
@@ -739,8 +719,6 @@
         moved[g * ROWS_DEV + moves[0, 0, g]] = lengths[right * ROWS_DEV + moves[0, 1, right]] + 1
         moved[g * ROWS_DEV + moves[0, 1, g]] = lengths[left * ROWS_DEV + moves[0, 0, left]] + 1
 
-    pass_on(3, ROWS_DEV + 1)
-
     @pl.loop(0, GROUPS)
     def _(g):
         for j in range(ROWS_DEV):
@@ -760,25 +738,23 @@
 def finish(lengths, moves, group, ordered, rows):
     smem = pl.BlockSpec(memory_space=pltpu.SMEM)
     hbm = pl.BlockSpec(memory_space=pltpu.HBM)
+    vmem = pl.BlockSpec(memory_space=pltpu.VMEM)
     return pl.pallas_call(
         finish_kernel,
         out_shape=(
-            jax.ShapeDtypeStruct(ordered.shape, ordered.dtype),
+            jax.ShapeDtypeStruct((ROWS_DEV, *ordered[0].shape), ordered[0].dtype),
             jax.ShapeDtypeStruct(rows.shape, rows.dtype),
             jax.ShapeDtypeStruct(lengths.shape, jnp.int32),
         ),
-        in_specs=[smem, smem, smem, hbm, hbm],
+        in_specs=[smem, smem, smem, vmem] + [vmem] * ROWS_DEV,
         out_specs=(hbm, hbm, smem),
         scratch_shapes=[
             pltpu.SMEM(lengths.shape, jnp.int32),
-            pltpu.VMEM(ordered.shape, ordered.dtype),
-            pltpu.VMEM(rows.shape, rows.dtype),
-            pltpu.SemaphoreType.DMA((2, ROWS_DEV)),
-            pltpu.SemaphoreType.DMA((2,)),
+            pltpu.SemaphoreType.DMA((ROWS_DEV + 1,)),
         ],
-        compiler_params=pltpu.CompilerParams(vmem_limit_bytes=60 * 1024 * 1024),
+        compiler_params=pltpu.CompilerParams(vmem_limit_bytes=8 * 1024 * 1024),
         name="finish",
-    )(lengths, moves, group, ordered, rows)
+    )(lengths, moves, group, rows, *ordered)
 
 
 def on_device(
@@ -796,7 +772,7 @@
     down_weight,
 ):
     moves = jnp.swapaxes(slot_moves, 1, 2)
-    rows, ordered = layer(
+    rows, *ordered = layer(
         lengths,
         moves,
         hidden_in.reshape(OWN, WIDTH),

time: 101 us -> 101 us (level)
  Pallas kernels: 100 us -> 97 us
  local copies, waits for them, and re-layouts: 0 us -> 2.87 us
    unnamed x0 -> x8, local copies, waits for them, and re-layouts: none -> 2.87 us
    pallas_call x1, Pallas kernels: 5.35 us -> 3.4 us  [finish(): pl.pallas_call(finish_kernel, out_shape=(jax.ShapeDtypeStruct((ROWS_DEV,...]
    pallas_call x1, Pallas kernels: 94.8 us -> 93.6 us  [layer(): pl.pallas_call(kernel, out_shape=(jax.ShapeDtypeStruct((OWN, WIDTH), bf16...]
where the time goes in v4:
time: 101 us
  Pallas kernels  97 us (96%)
  local copies, waits for them, and re-layouts  2.87 us (3%)
    pallas_call x1, Pallas kernels, layer(): pl.pallas_call(kernel, out_shape=(jax.ShapeDtypeStruct((OWN, WIDTH), bf16...  93.6 us
    pallas_call x1, Pallas kernels, finish(): pl.pallas_call(finish_kernel, out_shape=(jax.ShapeDtypeStruct((ROWS_DEV,...  3.4 us
    unnamed x8, local copies, waits for them, and re-layouts  2.87 us

profile of v4, /device:TPU:1, one launch (start us, length us, event | category | flops | bytes accessed | tf_op | source)
XLA Modules:
  0.0 100.7 jit_solution(12793560627248813826)
XLA Ops:
  0.6 0.0 copy-start
  0.6 0.8 copy-done
  1.5 0.0 copy-start.1
  1.5 0.7 copy-done.1
  2.2 0.0 copy-start.2
  2.2 0.7 copy-done.2
  2.8 0.0 copy-start.3
  2.8 0.7 copy-done.3
  3.5 93.6 %layer.1 = (bf16[16,1792]{1,0:T(8,128)(2,1)S(1)}, bf16[448,576]{1,0:T(8,128)(2,1)S(1)}, bf16[448,576]{1,0:T(8,128)(2,1)S(1)}, bf16[448,576]{1,0:T(8,128)(2,1)S(1...) custom-call(s32[256]{0:T(256)S(1)} %copy-done.3, ...), custom_call_target="tpu_custom_call" | custom-call | tf_op jit(solution)/shard_map/layer/pallas_call | solution.py:683
  97.2 3.4 %finish.1 = (bf16[8,448,576]{2,1,0:T(8,128)(2,1)}, bf16[16,1792]{1,0:T(8,128)(2,1)}, s32[256]{0:T(256)}) custom-call(s32[256]{0:T(256)S(1)} %copy-done.3, s32[2,2,32]{2,1,0:T(2,128)S(1)} %bitcast.9, s32[1]{0:T(128)} %bitcast.1.group, bf16[16,1792]{1,0:T(8,128)(2,1)S(1)} %get-tuple-element.15.rows, bf16[448,576]{1,0:T(8,128)(2,1)S(1)} %get-tuple-element.16.refs_0_, ...), custom_call_target="tpu_custom_call" | custom-call | tf_op jit(solution)/shard_map/finish/pallas_call | solution.py:742
Async XLA Ops:
  0.6 0.8 copy-start
  1.5 0.7 copy-start.1
  2.2 0.7 copy-start.2
  2.8 0.7 copy-start.3

commit v5 on v3

--- a/solution.py
+++ b/solution.py
@@ -224,13 +224,13 @@
             r.heads.at[step, k],
             r.head_rows.at[step, place],
             r.head_send.at[step, i],
-            r.head_recv.at[step, place],
+            r.head_recv.at[step],
             {"dp": here.x * (2 * N) + k, "tp": x},
         )
 
     def local():
         return pltpu.make_async_copy(
-            r.heads.at[step, k], r.head_rows.at[step, place], r.head_recv.at[step, place]
+            r.heads.at[step, k], r.head_rows.at[step, place], r.head_recv.at[step]
         )
 
     return kept, copy, local
@@ -471,18 +471,7 @@
 def back_line(here, r, step):
     f32, bf16 = jnp.float32, jnp.bfloat16
 
-    @pl.loop(0, GROUPS)
-    def _(i):
-        pltpu.make_async_copy(r.heads.at[step, 0], r.head_rows.at[step, i], r.head_recv.at[step, i]).wait()
-
-    @pl.loop(0, GROUPS)
-    def _(i):
-        kept, copy, _ = head_copy(here, r, step, i)
-
-        @pl.when(jnp.logical_not(kept))
-        def _():
-            copy().wait_send()
-
+    pltpu.make_async_copy(r.head_rows.at[step], r.head_rows.at[step], r.head_recv.at[step]).wait()
     rows = r.head_rows[step].astype(f32)
     for h in range(N):
         first = h % 2 * ROWS_DEV
@@ -496,13 +485,13 @@
         return ref[pl.ds(pl.multiple_of(c * HALF, HALF), HALF), :]
 
     project_both(here, r, step, 0, lambda c: half(r.head_block, c), r.wo[...])
-    yield
-    attention = yield from reduce_over_groups(here, r, step, 0)
     for i in range(ROWS_DEV):
         token = i // EARLY * ROWS_DEV + r.slots[step * EARLY + i % EARLY]
         r.line_tokens[step, i : i + 1, :] = r.tokens_wide[pl.ds(token, 1), :]
-    tokens = stacked(r.line_tokens[step])[0]
-    mixed = (tokens + attention).astype(bf16).astype(f32)
+    r.mixed[step] = stacked(r.line_tokens[step])[0]
+    yield
+    attention = yield from reduce_over_groups(here, r, step, 0)
+    mixed = (r.mixed[step] + attention).astype(bf16).astype(f32)
     r.mixed[step] = mixed
 
     mixed_all = r.mixed_all.at[step]
@@ -512,6 +501,15 @@
     copies = {}
     for o in reversed(CHIPS):
         copies[o] = send(mine, mine, sem.at[0, o], sem.at[1, o], here.on_chip(*here.chip(o)))
+
+    @pl.loop(0, GROUPS)
+    def _(i):
+        kept, copy, _ = head_copy(here, r, step, i)
+
+        @pl.when(jnp.logical_not(kept))
+        def _():
+            copy().wait_send()
+
     yield
     handed = []
     for o in (0, *NEAR_FIRST):
@@ -679,7 +677,7 @@
         move1_sem=dma(2, 2, MOVE_PARTS),
         out_sem=dma(ROWS_DEV),
         head_send=dma(STEPS, GROUPS),
-        head_recv=dma(STEPS, GROUPS),
+        head_recv=dma(STEPS),
         core_sem=dma(2, STEPS, 2),
         sum_sem=dma(2, STEPS, 2, BLOCKS),
         gather_sem=dma(STEPS, 2, BLOCKS),

time: 101 us -> 99.9 us (0.989)
  Pallas kernels: 100 us -> 98.9 us
    pallas_call x1, Pallas kernels: 94.8 us -> 93.5 us  [layer(): pl.pallas_call(kernel, out_shape=(jax.ShapeDtypeStruct((OWN, WIDTH), bf16...]
where the time goes in v5:
time: 99.9 us; the launch traced here: 99.7 us
  Pallas kernels  98.9 us (99%)
    pallas_call x1, Pallas kernels, layer(): pl.pallas_call(kernel, out_shape=(jax.ShapeDtypeStruct((OWN, WIDTH), bf16...  93.5 us
    pallas_call x1, Pallas kernels, finish(): pl.pallas_call(finish_kernel, out_shape=(jax.ShapeDtypeStruct(ordered.sha...  5.35 us

profile of v5, /device:TPU:1, one launch (start us, length us, event | category | flops | bytes accessed | tf_op | source)
XLA Modules:
  0.0 99.7 jit_solution(6274304477881250773)
XLA Ops:
  0.6 93.5 %layer.1 = (bf16[16,1792]{1,0:T(8,128)(2,1)}, bf16[8,448,576]{2,1,0:T(8,128)(2,1)}) custom-call(s32[256]{0:T(256)} %lengths.1, s32[2,2,32]{2,1,0:T(2,128)} %bitcast.11, bf16[16,1792]{1,0:T(8,128)(2,1)} %bitcast.10, f32[1792]{0:T(1024)} %refs_3_.1, bf16[576,1792]{1,0:T(8,128)(2,1)} %bitcast.7, bf16[2,8,32,576]{3,2,1,0:T(8,128)(2,1)} %refs_5_.1, ...), custom_call_target="tpu_custom_call" | custom-call | tf_op jit(solution)/shard_map/layer/pallas_call | solution.py:694
  94.2 5.4 %finish.1 = (bf16[8,448,576]{2,1,0:T(8,128)(2,1)}, bf16[16,1792]{1,0:T(8,128)(2,1)}, s32[256]{0:T(256)}) custom-call(s32[256]{0:T(256)} %lengths.1, s32[2,2,32]{2,1,0:T(2,128)} %bitcast.12, s32[1]{0:T(128)} %bitcast.1.group, bf16[8,448,576]{2,1,0:T(8,128)(2,1)} %get-tuple-element.8.ordered, bf16[16,1792]{1,0:T(8,128)(2,1)} %get-tuple-element.9.rows), custom_call_target="tpu_custom_call" | custom-call | tf_op jit(solution)/shard_map/finish/pallas_call | solution.py:761

commit v6 on v5

--- a/solution.py
+++ b/solution.py
@@ -89,6 +89,10 @@
     return copy
 
 
+def wait_all(block, sem):
+    pltpu.make_async_copy(block, block, sem).wait()
+
+
 def stacked(rows):
     left = rows[:, :COLS].reshape(-1, ROWS_DEV, COLS)
     right = rows[:, COLS:].reshape(-1, ROWS_DEV, COLS)
@@ -444,18 +448,19 @@
     sem = r.sum_sem.at[use, step]
     sums, rows = r.sums.at[step], r.rows.at[use, step]
     r.core_copy[use, step].wait()
-    copies = {}
     for o in reversed(CHIPS):
         y, z = here.chip(o)
         k = y * N + z
         sums[k] = (own[k].astype(jnp.float32) + peer[k].astype(jnp.float32)).astype(jnp.bfloat16)
-        copies[o] = send(sums.at[k], rows.at[o], sem.at[0, o], sem.at[1, o], here.on_chip(y, z))
+        send(sums.at[k], rows.at[o], sem.at[0, 0], sem.at[1, 0], here.on_chip(y, z))
     k = here.y * N + here.z
     total = own[k].astype(jnp.float32) + peer[k].astype(jnp.float32)
     yield
+    arrivals = rows.at[pl.ds(1, BLOCKS - 1)]
+    wait_all(arrivals, sem.at[1, 0])
     for o in CHIPS:
-        copies[o].wait()
         total = total + rows[o].astype(jnp.float32)
+    wait_all(arrivals, sem.at[0, 0])
     return total
 
 
@@ -498,9 +503,8 @@
     mine = mixed_all.at[here.c, here.y, here.z]
     mine[...] = mixed.astype(bf16)
     sem, core_sem = r.gather_sem.at[step], r.gather_core.at[step]
-    copies = {}
     for o in reversed(CHIPS):
-        copies[o] = send(mine, mine, sem.at[0, o], sem.at[1, o], here.on_chip(*here.chip(o)))
+        send(mine, mine, sem.at[0, 0], sem.at[1, o // N], here.on_chip(*here.chip(o)))
 
     @pl.loop(0, GROUPS)
     def _(i):
@@ -513,11 +517,12 @@
     yield
     handed = []
     for o in (0, *NEAR_FIRST):
-        for i in range(N):
-            if o + i:
-                copies[o * N + i].wait()
-        block = mixed_all.at[here.c, lax.rem(here.y + N - o, N)]
+        y = lax.rem(here.y + N - o, N)
+        block = mixed_all.at[here.c, y]
+        wait_all(block if o else mixed_all.at[here.c, y, pl.ds(0, N - 1)], sem.at[1, o])
         handed.append(send(block, block, core_sem.at[0, o], core_sem.at[1, o], here.on_core()))
+
+    wait_all(r.rows.at[0, step, pl.ds(1, BLOCKS - 1)], sem.at[0, 0])
 
     if step == 0:
         r.loads["wg"].wait()

time: 99.9 us -> 99.8 us (level)
  no operation moved by 1% of the time
where the time goes in v6:
time: 99.8 us; the launch traced here: 99.6 us
  Pallas kernels  98.8 us (99%)
    pallas_call x1, Pallas kernels, layer(): pl.pallas_call(kernel, out_shape=(jax.ShapeDtypeStruct((OWN, WIDTH), bf16...  93.5 us
    pallas_call x1, Pallas kernels, finish(): pl.pallas_call(finish_kernel, out_shape=(jax.ShapeDtypeStruct(ordered.sha...  5.35 us

profile of v6, /device:TPU:1, one launch (start us, length us, event | category | flops | bytes accessed | tf_op | source)
XLA Modules:
  0.0 99.6 jit_solution(14036434051866018244)
XLA Ops:
  0.6 93.5 %layer.1 = (bf16[16,1792]{1,0:T(8,128)(2,1)}, bf16[8,448,576]{2,1,0:T(8,128)(2,1)}) custom-call(s32[256]{0:T(256)} %lengths.1, s32[2,2,32]{2,1,0:T(2,128)} %bitcast.11, bf16[16,1792]{1,0:T(8,128)(2,1)} %bitcast.10, f32[1792]{0:T(1024)} %refs_3_.1, bf16[576,1792]{1,0:T(8,128)(2,1)} %bitcast.7, bf16[2,8,32,576]{3,2,1,0:T(8,128)(2,1)} %refs_5_.1, ...), custom_call_target="tpu_custom_call" | custom-call | tf_op jit(solution)/shard_map/layer/pallas_call | solution.py:699
  94.1 5.4 %finish.1 = (bf16[8,448,576]{2,1,0:T(8,128)(2,1)}, bf16[16,1792]{1,0:T(8,128)(2,1)}, s32[256]{0:T(256)}) custom-call(s32[256]{0:T(256)} %lengths.1, s32[2,2,32]{2,1,0:T(2,128)} %bitcast.12, s32[1]{0:T(128)} %bitcast.1.group, bf16[8,448,576]{2,1,0:T(8,128)(2,1)} %get-tuple-element.8.ordered, bf16[16,1792]{1,0:T(8,128)(2,1)} %get-tuple-element.9.rows), custom_call_target="tpu_custom_call" | custom-call | tf_op jit(solution)/shard_map/finish/pallas_call | solution.py:766
